TPU v7x, 32 devices: a whole 2x2x4 slice. The times are simulated.
32 devices in a mesh: seq: 8 (over z, x), head: 4 (over y, core).
Axes of the slice: x: 2, y: 2, z: 4, core: 2. Of those that a mesh axis runs over, the one named last changes fastest.
Arguments:
- tokens: bfloat16 [64, 1024, 768], P('seq', 'head'), may hold values from -1.1953125 to 1.1953125
- cotangent: bfloat16 [64, 1024, 768], P('seq', 'head'), may hold values from -6 to 6
- lengths: int32 [64], P('seq'), may hold values from 0 to 1024, as said below
- owners: int32 [64], P('seq'), may hold values from 0 to 7, as said below
- codons: int32 [64, 1024], P('seq'), may hold values from 0 to 63
- ln1_gain: bfloat16 [768], P('head'), may hold values from 0.5 to 1.5
- ln1_bias: bfloat16 [768], P('head'), may hold values from -1.75 to 1.75
- w_query: bfloat16 [768, 768], P('head'), may hold values from -0.21875 to 0.21875
- b_query: bfloat16 [768], P('head'), may hold values from -1.75 to 1.75
- w_key: bfloat16 [768, 768], P('head'), may hold values from -0.21875 to 0.21875
- b_key: bfloat16 [768], P('head'), may hold values from -1.75 to 1.75
- w_value: bfloat16 [768, 768], P('head'), may hold values from -0.21875 to 0.21875
- b_value: bfloat16 [768], P('head'), may hold values from -1.75 to 1.75
- w_out: bfloat16 [768, 768], P('head'), may hold values from -0.3125 to 0.3125
- b_out: bfloat16 [768], P('head'), may hold values from -1.75 to 1.75
- ln2_gain: bfloat16 [768], P('head'), may hold values from 0.5 to 1.5
- ln2_bias: bfloat16 [768], P('head'), may hold values from -1.75 to 1.75
- w_up: bfloat16 [768, 3072], P(None, 'head'), may hold values from -0.5 to 0.5
- b_up: bfloat16 [3072], P('head'), may hold values from -1.75 to 1.75
- w_down: bfloat16 [3072, 768], P('head'), may hold values from -0.3125 to 0.3125
- b_down: bfloat16 [768], P('head'), may hold values from -1.75 to 1.75
Outputs:
- mixed: bfloat16 [64, 1024, 768], P('seq', 'head')
- input_grad: bfloat16 [64, 1024, 768], P('seq', 'head')
- grad_ln1_gain: float32 [768], P('head')
- grad_ln1_bias: float32 [768], P('head')
- grad_w_query: float32 [768, 768], P('head')
- grad_b_query: float32 [768], P('head')
- grad_w_key: float32 [768, 768], P('head')
- grad_b_key: float32 [768], P('head')
- grad_w_value: float32 [768, 768], P('head')
- grad_b_value: float32 [768], P('head')
- grad_w_out: float32 [768, 768], P('head')
- grad_b_out: float32 [768], P('head')
- second_layer_norm_gain_gradient: float32 [768], P('head')
- grad_ln2_bias: float32 [768], P('head')
- grad_w_up: float32 [768, 3072], P(None, 'head')
- grad_b_up: float32 [3072], P('head')
- grad_w_down: float32 [3072, 768], P('head')
- grad_b_down: float32 [768], P('head')
- histogram: int32 [8, 64], P('seq')
Inputs may be any that keep to these rules, and one draw needn't show every extreme that they name: `lengths`: A device's sequences of nonzero length stand in its first slots and empty slots have length 0; on the first device of each group of 8 all 8 slots hold a sequence, and some sequence has 1024 codons. The sequences of nonzero length on one device go to distinct owners whose index // 8 equals the device's index // 8, and every owner receives exactly 4 of them.
All inputs are finite; a program needn't handle non-finite values.
Results may differ from a plain program's by a relative error of at most 0.015.
Values may be sent and summed in bfloat16 or wider, within the bound.
No kernel may reach another device: no remote copies, remote signals or barrier semaphores. Data moves between devices by JAX's collectives and lax.ppermute only.
A program may use at most 320 MiB of HBM per device.

v0:
```python
import jax
import jax.numpy as jnp
from jax import lax
from jax.sharding import PartitionSpec as P

HD = 64
CODONS = 64
GROUP = 8


EPSILON = 1e-05
NEGATIVE = -1e30


def prefix(array, axis, combine, identity):
    peers, here = (lax.axis_size(axis), lax.axis_index(axis))
    everything = lax.all_gather(array, axis)
    start = jnp.broadcast_to(jnp.asarray(identity, array.dtype), array.shape)

    def step(k, before):
        reached = k < here
        new = combine(before, everything[k])
        return jnp.where(reached, new, before)

    return lax.fori_loop(0, peers, step, start)


def partner(array, axis, bit):
    return lax.ppermute(array, axis, [(i, i ^ 1 << bit) for i in range(lax.axis_size(axis))])


def rotary_tables(sequence_length, size):
    half_size = size // 2
    frequency = 10000.0 ** (-(jnp.arange(half_size, dtype=jnp.float32) * 2.0 / size))
    angles = jnp.arange(sequence_length, dtype=jnp.float32)[:, None] * frequency[None, :]
    return (jnp.cos(angles), jnp.sin(angles))


def rotate(values, cos_table, sin_table):
    half_size = values.shape[-1] // 2
    former = values[..., :half_size]
    latter = values[..., half_size:]
    cos_part = cos_table[:, None, :]
    sin_part = sin_table[:, None, :]
    return jnp.concatenate(
        [former * cos_part - latter * sin_part, latter * cos_part + former * sin_part], axis=-1
    )


def add_counts(earlier, later):
    return earlier + later


def gelu_exact(values):
    return jax.nn.gelu(values, approximate=False)


def owned_row_section(flat, count, sequence_length, start, rows):
    shaped = flat.reshape(count, sequence_length, flat.shape[-1])
    return lax.dynamic_slice_in_dim(shaped, start, rows, 1).reshape(count * rows, flat.shape[-1])


def butterfly(buffers, mover):
    position = lax.axis_index("seq")
    sections = GROUP.bit_length() - 1
    for bit_number in range(sections):
        stride = 2**bit_number
        far_side = 1 - position // stride % 2
        results = []
        for buffer in buffers:
            trailing = buffer.shape[1:]
            shaped = buffer.reshape((GROUP // (2 * stride), 2, stride) + trailing)
            leaving = lax.dynamic_index_in_dim(shaped, far_side, 1, keepdims=False)
            arriving = mover(leaving.reshape((GROUP // 2,) + trailing), bit_number)
            shaped = lax.dynamic_update_index_in_dim(
                shaped, arriving.reshape(leaving.shape), far_side, 1
            )
            results.append(shaped.reshape(buffer.shape))
        buffers = tuple(results)
    return buffers


def attend(pieces):
    queries, key_rot, values, live_count = pieces
    scale_factor = HD ** (-0.5)
    scores = (
        jnp.einsum("qhd,khd->hqk", queries, key_rot, preferred_element_type=jnp.float32)
        * scale_factor
    )
    live_keys = jnp.arange(queries.shape[0])[None, None, :] < live_count
    scores = jnp.where(live_keys, scores, NEGATIVE)
    top_score = jnp.max(scores, axis=-1, keepdims=True)
    weights = jnp.exp(scores - top_score)
    totals = jnp.sum(weights, axis=-1, keepdims=True)
    weights_low = (weights / totals).astype(jnp.bfloat16)
    context = jnp.einsum("hqk,khd->qhd", weights_low, values, preferred_element_type=jnp.float32)
    return (context, top_score[..., 0] + jnp.log(totals[..., 0]))


def attend_back(pieces):
    queries, key_rot, values, live_count, log_total, context_grad = pieces
    scale_factor = HD ** (-0.5)
    scores = (
        jnp.einsum("qhd,khd->hqk", queries, key_rot, preferred_element_type=jnp.float32)
        * scale_factor
    )
    live_keys = jnp.arange(queries.shape[0])[None, None, :] < live_count
    scores = jnp.where(live_keys, scores, NEGATIVE)
    weights = jnp.exp(scores - log_total[..., None])
    weights_low = weights.astype(jnp.bfloat16)
    value_grad = jnp.einsum(
        "hqk,qhd->khd", weights_low, context_grad, preferred_element_type=jnp.float32
    )
    weight_grad = jnp.einsum(
        "qhd,khd->hqk", context_grad, values, preferred_element_type=jnp.float32
    )
    weighted_sum = jnp.sum(weight_grad * weights, axis=-1, keepdims=True)
    score_grad = (weights * (weight_grad - weighted_sum)).astype(jnp.bfloat16)
    query_grad = (
        jnp.einsum("hqk,khd->qhd", score_grad, key_rot, preferred_element_type=jnp.float32)
        * scale_factor
    )
    key_grad = (
        jnp.einsum("hqk,qhd->khd", score_grad, queries, preferred_element_type=jnp.float32)
        * scale_factor
    )
    return (query_grad, key_grad, value_grad)


def local(
    tokens,
    cotangent,
    lengths,
    owners,
    codons,
    ln1_gain,
    ln1_bias,
    w_query,
    b_query,
    w_key,
    b_key,
    w_value,
    b_value,
    w_out,
    b_out,
    ln2_gain,
    ln2_bias,
    w_up,
    b_up,
    w_down,
    b_down,
):
    position = lax.axis_index("seq")
    group_base = position // GROUP * GROUP
    relative = jnp.arange(GROUP, dtype=jnp.int32)
    live_slot = lengths > 0
    routing = (owners[None, :] == (group_base + relative)[:, None]) & live_slot[None, :]
    routing_int = routing.astype(jnp.int32)
    routing_reduced_precision = routing.astype(jnp.bfloat16)
    send_lengths = jnp.sum(routing_int * lengths[None, :], axis=1)
    send_codons = jnp.sum(routing_int[:, :, None] * codons[None, :, :], axis=1)
    everyone = jnp.arange(lax.axis_size("seq"), dtype=jnp.int32)
    sends = jnp.sum(
        ((owners[None, :] == everyone[:, None]) & live_slot[None, :]).astype(jnp.int32), axis=1
    )
    earlier = prefix(sends, "seq", add_counts, jnp.zeros_like(sends))
    details = jnp.stack(
        [send_lengths, lax.dynamic_slice_in_dim(earlier, group_base, GROUP, 0)], axis=1
    )

    def move_info(payload, bit_number):
        return partner(payload, "seq", bit_number)

    got_codons, got_details = butterfly((send_codons, details), move_info)
    got_lengths = got_details[:, 0]
    arrived = (got_lengths > 0).astype(jnp.int32)
    got_slots = got_details[:, 1]
    send_rows = jnp.einsum(
        "xk,kry->xry", routing_reduced_precision, tokens, preferred_element_type=jnp.float32
    ).astype(jnp.bfloat16)
    send_grads = jnp.einsum(
        "xk,kry->xry", routing_reduced_precision, cotangent, preferred_element_type=jnp.float32
    ).astype(jnp.bfloat16)

    def move_rows(payload, bit_number):
        return partner(payload, "seq", bit_number)

    got_rows, got_grads = butterfly((send_rows, send_grads), move_rows)
    owned_row_count = tokens.shape[0] // 2
    slot_index = jnp.arange(owned_row_count, dtype=jnp.int32)
    placing = (got_slots[:, None] == slot_index[None, :]) & (arrived[:, None] > 0)
    placing_low = placing.astype(jnp.bfloat16)
    own_rows = jnp.einsum(
        "bk,bld->kld", placing_low, got_rows, preferred_element_type=jnp.float32
    ).astype(jnp.bfloat16)
    own_grads = jnp.einsum(
        "bk,bld->kld", placing_low, got_grads, preferred_element_type=jnp.float32
    ).astype(jnp.bfloat16)
    own_lengths = jnp.sum(placing.astype(jnp.int32) * got_lengths[:, None], axis=0).astype(
        jnp.int32
    )
    codon_length = codons.shape[1]
    live_source = jnp.arange(codon_length)[None, :] < got_lengths[:, None]
    codon_index = jnp.arange(CODONS, dtype=jnp.int32)
    matches = (got_codons[:, :, None] == codon_index[None, None, :]) & live_source[:, :, None]
    histogram = jnp.sum(matches.astype(jnp.int32), axis=(0, 1))[None, :]

    def spread_back(rows_block):
        return jnp.einsum(
            "bk,kld->bld", placing_low, rows_block, preferred_element_type=jnp.float32
        ).astype(jnp.bfloat16)

    (
        full_rows,
        full_grads,
        first_norm_gain,
        first_norm_bias,
        second_norm_gain,
        second_norm_bias,
        bias_out,
        bias_down,
    ) = (
        lax.all_gather(own_rows, "head", axis=1, tiled=True),
        lax.all_gather(own_grads, "head", axis=1, tiled=True),
        lax.all_gather(ln1_gain, "head", axis=0, tiled=True),
        lax.all_gather(ln1_bias, "head", axis=0, tiled=True),
        lax.all_gather(ln2_gain, "head", axis=0, tiled=True),
        lax.all_gather(ln2_bias, "head", axis=0, tiled=True),
        lax.all_gather(b_out, "head", axis=0, tiled=True),
        lax.all_gather(b_down, "head", axis=0, tiled=True),
    )
    portion_rows = tokens.shape[1]
    sequence_length = full_rows.shape[1]
    width = tokens.shape[2]
    part_width = ln1_gain.shape[0]
    part_total = owned_row_count * portion_rows
    first_row_position = lax.axis_index("head") * portion_rows
    column_start = lax.axis_index("head") * part_width
    live_part = (
        (first_row_position + jnp.arange(portion_rows))[None, :] < own_lengths[:, None]
    ).reshape(part_total, 1)
    inputs_part = own_rows.reshape(part_total, width).astype(jnp.float32)
    query_weight, key_weight, value_weight, out_weight, down_weight, up_weight = (
        w_query,
        w_key,
        w_value,
        w_out,
        w_down,
        w_up,
    )
    query_bias, key_bias, value_bias, up_bias = (b_query, b_key, b_value, b_up)
    work_rows, work_grads, work_lengths = (full_rows, full_grads, own_lengths)

    def owned_column_range(vector):
        return lax.dynamic_slice_in_dim(vector, column_start, part_width, 0)

    row_total = owned_row_count * sequence_length
    live_flat = (jnp.arange(sequence_length)[None, :] < work_lengths[:, None]).reshape(row_total, 1)
    inputs_full = work_rows.reshape(row_total, width).astype(jnp.float32)
    first_mean_removed = inputs_full - jnp.mean(inputs_full, axis=-1, keepdims=True)
    first_inverse_deviation = lax.rsqrt(
        jnp.mean(first_mean_removed * first_mean_removed, axis=-1, keepdims=True) + EPSILON
    )
    first_standardized = first_mean_removed * first_inverse_deviation
    first_normalized_rows = (
        first_standardized * first_norm_gain.astype(jnp.float32)
        + first_norm_bias.astype(jnp.float32)
    ).astype(jnp.bfloat16)
    local_heads = query_weight.shape[0] // HD
    cos_table, sin_table = rotary_tables(sequence_length, HD)
    query_pre = jnp.einsum(
        "rd,ad->ra", first_normalized_rows, query_weight, preferred_element_type=jnp.float32
    ) + query_bias.astype(jnp.float32)
    key_pre = jnp.einsum(
        "rd,ad->ra", first_normalized_rows, key_weight, preferred_element_type=jnp.float32
    ) + key_bias.astype(jnp.float32)
    queries = rotate(
        query_pre.reshape(owned_row_count, sequence_length, local_heads, HD), cos_table, sin_table
    ).astype(jnp.bfloat16)
    key_rot = rotate(
        key_pre.reshape(owned_row_count, sequence_length, local_heads, HD), cos_table, sin_table
    ).astype(jnp.bfloat16)
    values = (
        (
            jnp.einsum(
                "rd,ad->ra", first_normalized_rows, value_weight, preferred_element_type=jnp.float32
            )
            + value_bias.astype(jnp.float32)
        )
        .astype(jnp.bfloat16)
        .reshape(owned_row_count, sequence_length, local_heads, HD)
    )
    contexts, log_totals = lax.map(attend, (queries, key_rot, values, work_lengths))
    context_low = contexts.reshape(row_total, local_heads * HD).astype(jnp.bfloat16)
    attention_part = jnp.dot(context_low, out_weight, preferred_element_type=jnp.float32)
    attention_share = lax.psum_scatter(
        attention_part.reshape(owned_row_count, sequence_length, width),
        "head",
        scatter_dimension=1,
        tiled=True,
    ).reshape(part_total, width)
    middle_part = inputs_part + attention_share + bias_out.astype(jnp.float32)
    middle_full = lax.all_gather(
        middle_part.reshape(owned_row_count, portion_rows, width), "head", axis=1, tiled=True
    ).reshape(row_total, width)
    second_mean_removed = middle_full - jnp.mean(middle_full, axis=-1, keepdims=True)
    second_inverse_deviation = lax.rsqrt(
        jnp.mean(second_mean_removed * second_mean_removed, axis=-1, keepdims=True) + EPSILON
    )
    second_standardized = second_mean_removed * second_inverse_deviation
    second_normalized_rows = (
        second_standardized * second_norm_gain.astype(jnp.float32)
        + second_norm_bias.astype(jnp.float32)
    ).astype(jnp.bfloat16)
    hidden_pre = jnp.dot(
        second_normalized_rows, up_weight, preferred_element_type=jnp.float32
    ) + up_bias.astype(jnp.float32)
    hidden_low = gelu_exact(hidden_pre).astype(jnp.bfloat16)
    down_part = jnp.dot(hidden_low, down_weight, preferred_element_type=jnp.float32)
    down_share = lax.psum_scatter(
        down_part.reshape(owned_row_count, sequence_length, width),
        "head",
        scatter_dimension=1,
        tiled=True,
    ).reshape(part_total, width)
    output_part = jnp.where(
        live_part, middle_part + down_share + bias_down.astype(jnp.float32), 0.0
    ).astype(jnp.bfloat16)
    output_rows = output_part.reshape(owned_row_count, portion_rows, width)
    out_grad = jnp.where(live_flat, work_grads.reshape(row_total, width).astype(jnp.float32), 0.0)
    out_grad_low = out_grad.astype(jnp.bfloat16)
    grad_b_down = owned_column_range(jnp.sum(out_grad, axis=0))
    grad_w_down = jnp.einsum(
        "rf,rd->fd", hidden_low, out_grad_low, preferred_element_type=jnp.float32
    )
    hidden_grad = jnp.einsum(
        "rd,fd->rf", out_grad_low, down_weight, preferred_element_type=jnp.float32
    )
    _, gelu_pull = jax.vjp(gelu_exact, hidden_pre)
    pre_grad = gelu_pull(hidden_grad)[0]
    grad_b_up = jnp.sum(pre_grad, axis=0)
    pre_grad_low = pre_grad.astype(jnp.bfloat16)
    grad_w_up = jnp.einsum(
        "rd,rf->df", second_normalized_rows, pre_grad_low, preferred_element_type=jnp.float32
    )
    norm_two_part = jnp.einsum(
        "rf,df->rd", pre_grad_low, up_weight, preferred_element_type=jnp.float32
    )
    second_norm_gradient = lax.psum(norm_two_part, "head")
    second_gain_scaled = second_norm_gradient * second_norm_gain.astype(jnp.float32)
    second_layer_norm_gain_gradient = owned_column_range(
        jnp.sum(second_norm_gradient * second_standardized, axis=0)
    )
    grad_ln2_bias = owned_column_range(jnp.sum(second_norm_gradient, axis=0))
    middle_grad = out_grad + second_inverse_deviation * (
        second_gain_scaled
        - jnp.mean(second_gain_scaled, axis=-1, keepdims=True)
        - second_standardized
        * jnp.mean(second_gain_scaled * second_standardized, axis=-1, keepdims=True)
    )
    middle_grad_low = middle_grad.astype(jnp.bfloat16)
    grad_b_out = owned_column_range(jnp.sum(middle_grad, axis=0))
    grad_w_out = jnp.einsum(
        "ra,rd->ad", context_low, middle_grad_low, preferred_element_type=jnp.float32
    )
    context_grad = (
        jnp.einsum("rd,ad->ra", middle_grad_low, out_weight, preferred_element_type=jnp.float32)
        .astype(jnp.bfloat16)
        .reshape(owned_row_count, sequence_length, local_heads, HD)
    )
    query_grad, key_grad, value_grad = lax.map(
        attend_back, (queries, key_rot, values, work_lengths, log_totals, context_grad)
    )
    query_pre_grad = rotate(query_grad, cos_table, -sin_table).reshape(row_total, local_heads * HD)
    key_pre_grad = rotate(key_grad, cos_table, -sin_table).reshape(row_total, local_heads * HD)
    value_pre_grad = value_grad.reshape(row_total, local_heads * HD)
    grad_b_query = jnp.sum(query_pre_grad, axis=0)
    grad_b_key = jnp.sum(key_pre_grad, axis=0)
    grad_b_value = jnp.sum(value_pre_grad, axis=0)
    query_low = query_pre_grad.astype(jnp.bfloat16)
    key_low = key_pre_grad.astype(jnp.bfloat16)
    value_low = value_pre_grad.astype(jnp.bfloat16)
    grad_w_query = jnp.einsum(
        "ra,rd->ad", query_low, first_normalized_rows, preferred_element_type=jnp.float32
    )
    grad_w_key = jnp.einsum(
        "ra,rd->ad", key_low, first_normalized_rows, preferred_element_type=jnp.float32
    )
    grad_w_value = jnp.einsum(
        "ra,rd->ad", value_low, first_normalized_rows, preferred_element_type=jnp.float32
    )
    norm_one_part = jnp.einsum(
        "ra,ad->rd", query_low, query_weight, preferred_element_type=jnp.float32
    )
    norm_one_part = norm_one_part + jnp.einsum(
        "ra,ad->rd", key_low, key_weight, preferred_element_type=jnp.float32
    )
    norm_one_part = norm_one_part + jnp.einsum(
        "ra,ad->rd", value_low, value_weight, preferred_element_type=jnp.float32
    )
    first_norm_portion = lax.psum_scatter(
        norm_one_part.reshape(owned_row_count, sequence_length, width),
        "head",
        scatter_dimension=1,
        tiled=True,
    ).reshape(part_total, width)
    first_standardized_portion = owned_row_section(
        first_standardized, owned_row_count, sequence_length, first_row_position, portion_rows
    )
    rstd_one_part = owned_row_section(
        first_inverse_deviation, owned_row_count, sequence_length, first_row_position, portion_rows
    )
    middle_grad_part = owned_row_section(
        middle_grad, owned_row_count, sequence_length, first_row_position, portion_rows
    )
    first_gain_scaled = first_norm_portion * first_norm_gain.astype(jnp.float32)
    input_grad_part = middle_grad_part + rstd_one_part * (
        first_gain_scaled
        - jnp.mean(first_gain_scaled, axis=-1, keepdims=True)
        - first_standardized_portion
        * jnp.mean(first_gain_scaled * first_standardized_portion, axis=-1, keepdims=True)
    )
    grad_ln1_gain, grad_ln1_bias = (
        lax.psum_scatter(
            jnp.sum(first_norm_portion * first_standardized_portion, axis=0),
            "head",
            scatter_dimension=0,
            tiled=True,
        ),
        lax.psum_scatter(
            jnp.sum(first_norm_portion, axis=0), "head", scatter_dimension=0, tiled=True
        ),
    )
    input_grad_rows = input_grad_part.astype(jnp.bfloat16).reshape(
        owned_row_count, portion_rows, width
    )
    gradients = lax.psum(
        (
            grad_ln1_gain,
            grad_ln1_bias,
            grad_w_query,
            grad_b_query,
            grad_w_key,
            grad_b_key,
            grad_w_value,
            grad_b_value,
            grad_w_out,
            grad_b_out,
            second_layer_norm_gain_gradient,
            grad_ln2_bias,
            grad_w_up,
            grad_b_up,
            grad_w_down,
            grad_b_down,
        ),
        "seq",
    )

    def move_both(payload, bit_number):
        return partner(payload, "seq", bit_number)

    output_gradient_return, input_gradient_return = butterfly(
        (spread_back(output_rows), spread_back(input_grad_rows)), move_both
    )
    mixed_out = jnp.einsum(
        "pt,pgz->tgz",
        routing_reduced_precision,
        output_gradient_return,
        preferred_element_type=jnp.float32,
    ).astype(jnp.bfloat16)
    input_out = jnp.einsum(
        "pt,pgz->tgz",
        routing_reduced_precision,
        input_gradient_return,
        preferred_element_type=jnp.float32,
    ).astype(jnp.bfloat16)
    return (mixed_out, input_out) + tuple(gradients) + (histogram,)


def solution(mesh):
    return jax.shard_map(
        local,
        mesh=mesh,
        in_specs=(
            P("seq", "head", None),
            P("seq", "head", None),
            P("seq"),
            P("seq"),
            P("seq", None),
            P("head"),
            P("head"),
            P("head", None),
            P("head"),
            P("head", None),
            P("head"),
            P("head", None),
            P("head"),
            P("head", None),
            P("head"),
            P("head"),
            P("head"),
            P(None, "head"),
            P("head"),
            P("head", None),
            P("head"),
        ),
        out_specs=(
            P("seq", "head", None),
            P("seq", "head", None),
            P("head"),
            P("head"),
            P("head", None),
            P("head"),
            P("head", None),
            P("head"),
            P("head", None),
            P("head"),
            P("head", None),
            P("head"),
            P("head"),
            P("head"),
            P(None, "head"),
            P("head"),
            P("head", None),
            P("head"),
            P("seq", None),
        ),
        check_vma=False,
    )
```

profile of v0, /device:TPU:0, one launch (start us, length us, event | category | flops | bytes accessed | tf_op | source)
XLA Modules:
  0.0 2238.1 jit_solution(5435617456937319669)
XLA Ops:
  27.0 34.7 %collective-permute-done.3 = bf16[4,256,768]{2,1,0:T(8,128)(2,1)} collective-permute-done((bf16[4,256,768]{2,1,0:T(8,128)(2,1)}, bf16[4,256,768]{2,1,0:T(8,128)(2,1)}, u32[]{:S(2)}, u32[]{:S(2)}) %collective-permute-start.3) | collective-permute-done | bytes 1572896 | tf_op jit(solution)/shard_map/ppermute | solution.py:29
  67.2 45.8 %dynamic_update_slice.83 = bf16[4,2,1,256,768]{4,1,0,3,2:T(2,128)(2,1)S(1)} dynamic-update-slice(bf16[4,2,1,256,768]{4,1,0,3,2:T(2,128)(2,1)S(1)} %reshape.688, bf16[4,1,1,256,768]{4,1,0,3,2:T(2,128)(2,1)} %copy.238, s32[]{:T(128)} %constant.322.clone.1, s32[]{:T(128)S(6)} %select_n.158, s32[]{:T(128)} %constant.322.clone.1, s32[]{:T(128)} %constant.322.clone.1, s32[]{:T(128)} %constant.322.clone.1) | dynamic-update-slice | bytes 3145732 | tf_op jit(solution)/shard_map/jit(dynamic_update_index_in_dim)/dynamic_update_slice | solution.py:75
  123.7 36.6 %all-reduce = s32[64]{0:T(128)S(1)} all-reduce(s32[64]{0:T(128)S(1)} %dynamic-update-slice), channel_id=2, replica_groups=mesh['seq'=8,'head'=4] {'seq'}, use_global_device_ids=true, to_apply=%add | all-reduce | flops 64 | bytes 512
  180.4 25.3 %collective-permute-done.1 = s32[4,2]{0,1:T(2,128)S(1)} collective-permute-done((s32[4,2]{0,1:T(2,128)S(1)}, s32[4,2]{0,1:T(2,128)S(1)}, u32[]{:S(2)}, u32[]{:S(2)}) %collective-permute-start.1) | collective-permute-done | bytes 64 | tf_op jit(solution)/shard_map/ppermute | solution.py:29
  210.4 31.5 %collective-permute-done.2 = s32[4,2]{0,1:T(2,128)S(1)} collective-permute-done((s32[4,2]{0,1:T(2,128)S(1)}, s32[4,2]{0,1:T(2,128)S(1)}, u32[]{:S(2)}, u32[]{:S(2)}) %collective-permute-start.2) | collective-permute-done | bytes 64 | tf_op jit(solution)/shard_map/ppermute | solution.py:29
  267.7 28.8 %all-gather.5.cloned.1.call-done = bf16[4,1024,768]{2,0,1:T(4,128)(2,1)} async-done(((bf16[4,256,768]{2,0,1:T(4,128)(2,1)}), bf16[4,1024,768]{2,0,1:T(4,128)(2,1)}) %all-gather.5.cloned.1.call-update) | async-done | bytes 6291472 | tf_op jit(solution)/shard_map/all_gather | solution.py:223
  346.9 49.5 %while.43 = (s32[]{:T(128)}, bf16[4,1024,3,64]{1,3,2,0:T(8,128)(2,1)}, f32[4,3,1024]{2,1,0:T(4,128)}, bf16[4,1024,3,64]{1,3,2,0:T(8,128)(2,1)}, s32[4]{0:T(128)S...) while((s32[]{:T(128)}, bf16[4,1024,3,64]{1,3,2,0:T(8,128)(2,1)}, ...), condition=%wide.region_10.11_spmd.clone, body=%wide.region_7.10_spmd.sunk.clone | while | flops 843053056 | bytes 52414624 | solution.py:293
  400.9 23.4 %copy.249 = f32[4,1024,768]{2,0,1:T(4,128)} copy(f32[4,1024,768]{2,1,0:T(8,128)S(1)} %fusion.98) | data formatting | bytes 25165824 | tf_op jit(solution)/shard_map/dot_general | solution.py:295
  441.3 35.1 %collective-permute-done.9 = bf16[4,256,768]{2,1,0:T(8,128)(2,1)S(1)} collective-permute-done((bf16[4,256,768]{2,1,0:T(8,128)(2,1)S(1)}, bf16[4,256,768]{2,1,0:T(8,128)(2,1)S(1)}, u32[]{:S(2)}, u32[]{:S(2)}) %collective-permute-start.9) | collective-permute-done | bytes 1572896 | tf_op jit(solution)/shard_map/ppermute | solution.py:29
  480.4 45.9 %dynamic_update_slice.89 = bf16[4,2,1,256,768]{4,1,0,3,2:T(2,128)(2,1)S(1)} dynamic-update-slice(bf16[4,2,1,256,768]{4,1,0,3,2:T(2,128)(2,1)S(1)} %reshape.703, bf16[4,1,1,256,768]{4,1,0,3,2:T(2,128)(2,1)} %copy.260, s32[]{:T(128)} %constant.322.clone.1, s32[]{:T(128)S(6)} %select_n.158, s32[]{:T(128)} %constant.322.clone.1, s32[]{:T(128)} %constant.322.clone.1, s32[]{:T(128)} %constant.322.clone.1) | dynamic-update-slice | bytes 3145732 | tf_op jit(solution)/shard_map/jit(dynamic_update_index_in_dim)/dynamic_update_slice | solution.py:75
  534.8 34.8 %collective-permute-done.10 = bf16[4,256,768]{2,0,1:T(4,128)(2,1)} collective-permute-done((bf16[4,256,768]{2,0,1:T(4,128)(2,1)}, bf16[4,256,768]{2,0,1:T(4,128)(2,1)}, u32[]{:S(2)}, u32[]{:S(2)}) %collective-permute-start.10) | collective-permute-done | bytes 1572896 | tf_op jit(solution)/shard_map/ppermute | solution.py:29
  584.4 67.3 %collective-permute-done.11 = bf16[4,256,768]{2,0,1:T(4,128)(2,1)S(1)} collective-permute-done((bf16[4,256,768]{2,0,1:T(4,128)(2,1)S(1)}, bf16[4,256,768]{2,0,1:T(4,128)(2,1)S(1)}, u32[]{:S(2)}, u32[]{:S(2)}) %collective-permute-start.11) | collective-permute-done | bytes 1572896 | tf_op jit(solution)/shard_map/ppermute | solution.py:29
  665.4 39.9 %all-gather.9.cloned.1.call-done = bf16[4,1024,768]{2,0,1:T(4,128)(2,1)} async-done(((bf16[4,256,768]{2,0,1:T(4,128)(2,1)}), bf16[4,1024,768]{2,0,1:T(4,128)(2,1)}) %all-gather.9.cloned.1.call-update) | async-done | bytes 6291472 | tf_op jit(solution)/shard_map/all_gather | solution.py:224
  718.1 71.3 %all-gather.7.cloned.1.call-done = f32[4,1024,768]{2,0,1:T(4,128)} async-done(((f32[4,256,768]{2,0,1:T(4,128)}), f32[4,1024,768]{2,0,1:T(4,128)}) %all-gather.7.cloned.1.call-update) | async-done | bytes 12582928 | tf_op jit(solution)/shard_map/all_gather | solution.py:303
  836.5 35.5 %fusion.133 = (f32[768]{0:T(1024)}, bf16[4096,768]{1,0:T(8,128)(2,1)}, f32[4096,768]{1,0:T(8,128)}) fusion(f32[4096,768]{1,0:T(8,128)S(1)} %fusion.142, f32[768]{0:T(1024)S(1)} %convert_element_type.218, bf16[4096,768]{1,0:T(8,128)(2,1)S(1)} %bitcast.405, bf16[768,768]{1,0:T(8,128)(2,1)S(1)} %copy-done.84), kind=kOutput, calls=%fused_computation.263 | convolution fusion | flops 5064621056 | bytes 38934528 | tf_op jit(solution)/shard_map/rd,fd->rf/dot_general | solution.py:336
  898.5 23.5 %copy.254 = f32[4,1024,768]{2,0,1:T(4,128)} copy(f32[4,1024,768]{2,1,0:T(8,128)S(1)} %bitcast.397) | data formatting | bytes 25165824 | tf_op jit(solution)/shard_map/reshape | solution.py:321
  922.0 181.4 %all-reduce.22.cloned.1.call-done = f32[4096,768]{1,0:T(8,128)} async-done(((f32[4096,768]{1,0:T(8,128)}), f32[4096,768]{1,0:T(8,128)}) %all-reduce.22.cloned.1.call-update) | async-done | bytes 12582928 | tf_op jit(solution)/shard_map/psum | solution.py:349
  1140.2 111.1 %while.44 = (s32[]{:T(128)}, f32[4,1024,3,64]{1,3,2,0:T(8,128)}, f32[4,1024,3,64]{1,3,2,0:T(8,128)}, f32[4,1024,3,64]{1,3,2,0:T(8,128)}, bf16[4,1024,3,64]{1,3,2...) while((s32[]{:T(128)}, f32[4,1024,3,64]{1,3,2,0:T(8,128)}, ...), condition=%wide.region_20.21_spmd.clone, body=%wide.region_18.20_spmd.sunk.clone | while | flops 2060843008 | bytes 124744864 | solution.py:371
  1341.9 382.4 %all-reduce.28.cloned.1.call-done = (f32[4,1024,768]{2,0,1:T(4,128)}, f32[4,1024,768]{2,0,1:T(4,128)}) async-done(((f32[4,1024,768]{2,0,1:T(4,128)}, f32[4,1024,768]{2,0,1:T(4,128)}), (f32[4,1024,768]{2,0,1:T(4,128)}, f32[4,1024,768]{2,0,1:T(4,128)})) %all-reduce.28.cloned.1.call-update) | async-done | bytes 25165840
  1769.0 30.9 %collective-permute-done.12 = bf16[4,256,768]{2,1,0:T(8,128)(2,1)} collective-permute-done((bf16[4,256,768]{2,1,0:T(8,128)(2,1)}, bf16[4,256,768]{2,1,0:T(8,128)(2,1)}, u32[]{:S(2)}, u32[]{:S(2)}) %collective-permute-start.12) | collective-permute-done | bytes 1572896 | tf_op jit(solution)/shard_map/ppermute | solution.py:29
  1805.4 45.8 %dynamic_update_slice.92 = bf16[4,2,1,256,768]{4,1,0,3,2:T(2,128)(2,1)S(1)} dynamic-update-slice(bf16[4,2,1,256,768]{4,1,0,3,2:T(2,128)(2,1)S(1)} %reshape.711, bf16[4,1,1,256,768]{4,1,0,3,2:T(2,128)(2,1)} %copy.271, s32[]{:T(128)} %constant.322.clone.1, s32[]{:T(128)S(6)} %select_n.158, s32[]{:T(128)} %constant.322.clone.1, s32[]{:T(128)} %constant.322.clone.1, s32[]{:T(128)} %constant.322.clone.1) | dynamic-update-slice | bytes 3145732 | tf_op jit(solution)/shard_map/jit(dynamic_update_index_in_dim)/dynamic_update_slice | solution.py:75
  1865.7 47.7 %dynamic_update_slice.86 = bf16[4,2,1,256,768]{4,1,0,3,2:T(2,128)(2,1)} dynamic-update-slice(bf16[4,2,1,256,768]{4,1,0,3,2:T(2,128)(2,1)} %reshape.698, bf16[4,1,1,256,768]{4,1,0,3,2:T(2,128)(2,1)} %copy.256, s32[]{:T(128)} %constant.322.clone.1, s32[]{:T(128)S(6)} %select_n.158, s32[]{:T(128)} %constant.322.clone.1, s32[]{:T(128)} %constant.322.clone.1, s32[]{:T(128)} %constant.322.clone.1) | dynamic-update-slice | bytes 3145732 | tf_op jit(solution)/shard_map/jit(dynamic_update_index_in_dim)/dynamic_update_slice | solution.py:75
  1929.0 93.3 %collective-permute-done.16 = s32[4,1024]{1,0:T(4,128)S(1)} collective-permute-done((s32[4,1024]{1,0:T(4,128)S(1)}, s32[4,1024]{1,0:T(4,128)S(1)}, u32[]{:S(2)}, u32[]{:S(2)}) %collective-permute-start.16) | collective-permute-done | bytes 16416 | tf_op jit(solution)/shard_map/ppermute | solution.py:29
  2076.3 124.2 %all-reduce.12 = (f32[192]{0:T(256)}, f32[192]{0:T(256)}, f32[192]{0:T(256)}, f32[192]{0:T(256)}, f32[192]{0:T(256)}, /*index=5*/f32[192]{0:T(256)}, f32[192]{0:...) all-reduce(f32[192]{0:T(256)S(1)} %dynamic-slice.18, ...), channel_id=1, replica_groups=mesh['seq'=8,'head'=4] {'seq'}, use_global_device_ids=true, to_apply=%region_26.27 | all-reduce | flops 2496 | bytes 19968 | tf_op jit(solution)/shard_map/psum | solution.py:437
  (584 shorter events, 733.0 us)
Async XLA Ops:
  7.2 289.3 %all-gather.5.cloned.1.call-start = ((), (), s32[]{:S(2)}) async-start(), calls=%async_computation | async-start | bytes 7864320 | tf_op jit(solution)/shard_map/all_gather | solution.py:223
  24.1 37.6 %collective-permute-start.3 = (bf16[4,256,768]{2,1,0:T(8,128)(2,1)}, bf16[4,256,768]{2,1,0:T(8,128)(2,1)}, u32[]{:S(2)}, u32[]{:S(2)}) collective-permute-start(bf16[4,256,768]{2,1,0:T(8,128)(2,1)} %bitcast.316), channel_id=1, source_target_pairs={{0,4},{4,0},{8,12},{12,8},{16,20},{20,16},{24,28},{28,24},{1,5},{5... | collective-permute-start | bytes 4718600 | tf_op jit(solution)/shard_map/ppermute | solution.py:29
  120.2 40.1 %collective-permute-start.4 = (bf16[4,256,768]{2,0,1:T(4,128)(2,1)}, bf16[4,256,768]{2,0,1:T(4,128)(2,1)}, u32[]{:S(2)}, u32[]{:S(2)}) collective-permute-start(bf16[4,256,768]{2,0,1:T(4,128)(2,1)} %reshape.690), channel_id=1, source_target_pairs={{0,8},{4,12},{8,0},{12,4},{16,24},{20,28},{24,16},{28,20},{1,9},{5... | collective-permute-start | bytes 4718600 | tf_op jit(solution)/shard_map/ppermute | solution.py:29
  173.5 68.7 %collective-permute-start.5 = (bf16[4,256,768]{2,0,1:T(4,128)(2,1)}, bf16[4,256,768]{2,0,1:T(4,128)(2,1)}, u32[]{:S(2)}, u32[]{:S(2)}) collective-permute-start(bf16[4,256,768]{2,0,1:T(4,128)(2,1)} %dynamic-slice_bitcast_fusion.4), channel_id=1, source_target_pairs={{0,16},{4,20},{8,24},{12,28},{16,0},{20,4},{24,8},{28,12},{1,17},{... | collective-permute-start | bytes 4718600 | tf_op jit(solution)/shard_map/ppermute | solution.py:29
  178.8 26.9 %collective-permute-start.1 = (s32[4,2]{0,1:T(2,128)S(1)}, s32[4,2]{0,1:T(2,128)S(1)}, u32[]{:S(2)}, u32[]{:S(2)}) collective-permute-start(s32[4,2]{0,1:T(2,128)S(1)} %reshape.685), channel_id=1, source_target_pairs={{0,8},{4,12},{8,0},{12,4},{16,24},{20,28},{24,16},{28,20},{1,9},{5... | collective-permute-start | bytes 104 | tf_op jit(solution)/shard_map/ppermute | solution.py:29
  206.4 35.5 %collective-permute-start.2 = (s32[4,2]{0,1:T(2,128)S(1)}, s32[4,2]{0,1:T(2,128)S(1)}, u32[]{:S(2)}, u32[]{:S(2)}) collective-permute-start(s32[4,2]{0,1:T(2,128)S(1)} %fusion.127), channel_id=1, source_target_pairs={{0,16},{4,20},{8,24},{12,28},{16,0},{20,4},{24,8},{28,12},{1,17},{... | collective-permute-start | bytes 104 | tf_op jit(solution)/shard_map/ppermute | solution.py:29
  250.9 408.8 %all-reduce.24.cloned.1.call-start = ((), (), s32[]{:S(2)}) async-start(), calls=%async_computation.4 | async-start | bytes 25165824
  424.3 281.0 %all-gather.9.cloned.1.call-start = ((), (), s32[]{:S(2)}) async-start(), calls=%async_computation.2 | async-start | bytes 7864320 | tf_op jit(solution)/shard_map/all_gather | solution.py:224
  439.7 36.6 %collective-permute-start.9 = (bf16[4,256,768]{2,1,0:T(8,128)(2,1)S(1)}, bf16[4,256,768]{2,1,0:T(8,128)(2,1)S(1)}, u32[]{:S(2)}, u32[]{:S(2)}) collective-permute-start(bf16[4,256,768]{2,1,0:T(8,128)(2,1)S(1)} %bitcast.420), channel_id=1, source_target_pairs={{0,4},{4,0},{8,12},{12,8},{16,20},{20,16},{24,28},{28,24},{1,5},{5... | collective-permute-start | bytes 4718600 | tf_op jit(solution)/shard_map/ppermute | solution.py:29
  533.4 36.2 %collective-permute-start.10 = (bf16[4,256,768]{2,0,1:T(4,128)(2,1)}, bf16[4,256,768]{2,0,1:T(4,128)(2,1)}, u32[]{:S(2)}, u32[]{:S(2)}) collective-permute-start(bf16[4,256,768]{2,0,1:T(4,128)(2,1)} %reshape.705), channel_id=1, source_target_pairs={{0,8},{4,12},{8,0},{12,4},{16,24},{20,28},{24,16},{28,20},{1,9},{5... | collective-permute-start | bytes 4718600 | tf_op jit(solution)/shard_map/ppermute | solution.py:29
  582.0 69.7 %collective-permute-start.11 = (bf16[4,256,768]{2,0,1:T(4,128)(2,1)S(1)}, bf16[4,256,768]{2,0,1:T(4,128)(2,1)S(1)}, u32[]{:S(2)}, u32[]{:S(2)}) collective-permute-start(bf16[4,256,768]{2,0,1:T(4,128)(2,1)S(1)} %dynamic-slice_bitcast_fusion.2), channel_id=1, source_target_pairs={{0,16},{4,20},{8,24},{12,28},{16,0},{20,4},{24,8},{28,12},{1,17},{... | collective-permute-start | bytes 4718600 | tf_op jit(solution)/shard_map/ppermute | solution.py:29
  658.9 130.6 %all-gather.7.cloned.1.call-start = ((), (), s32[]{:S(2)}) async-start(), calls=%async_computation.1 | async-start | bytes 15728640 | tf_op jit(solution)/shard_map/all_gather | solution.py:303
  664.1 439.3 %all-reduce.22.cloned.1.call-start = ((), (), s32[]{:S(2)}) async-start(), calls=%async_computation.3 | async-start | bytes 25165824 | tf_op jit(solution)/shard_map/psum | solution.py:349
  882.6 841.7 %all-reduce.28.cloned.1.call-start = ((), (), s32[]{:S(2)}) async-start(), calls=%async_computation.6 | async-start | bytes 50331648
  1300.3 920.0 %all-reduce.26.cloned.1.call-start = ((), (), s32[]{:S(2)}) async-start(), calls=%async_computation.5 | async-start | bytes 14155776 | tf_op jit(solution)/shard_map/psum | solution.py:437
  1747.4 52.5 %collective-permute-start.12 = (bf16[4,256,768]{2,1,0:T(8,128)(2,1)}, bf16[4,256,768]{2,1,0:T(8,128)(2,1)}, u32[]{:S(2)}, u32[]{:S(2)}) collective-permute-start(bf16[4,256,768]{2,1,0:T(8,128)(2,1)} %bitcast.313), channel_id=1, source_target_pairs={{0,4},{4,0},{8,12},{12,8},{16,20},{20,16},{24,28},{28,24},{1,5},{5... | collective-permute-start | bytes 4718600 | tf_op jit(solution)/shard_map/ppermute | solution.py:29
  1768.1 92.1 %collective-permute-start.6 = (bf16[4,256,768]{2,1,0:T(8,128)(2,1)}, bf16[4,256,768]{2,1,0:T(8,128)(2,1)}, u32[]{:S(2)}, u32[]{:S(2)}) collective-permute-start(bf16[4,256,768]{2,1,0:T(8,128)(2,1)} %bitcast.315), channel_id=1, source_target_pairs={{0,4},{4,0},{8,12},{12,8},{16,20},{20,16},{24,28},{28,24},{1,5},{5... | collective-permute-start | bytes 4718600 | tf_op jit(solution)/shard_map/ppermute | solution.py:29
  1858.6 167.5 %collective-permute-start.13 = (bf16[4,256,768]{2,0,1:T(4,128)(2,1)}, bf16[4,256,768]{2,0,1:T(4,128)(2,1)}, u32[]{:S(2)}, u32[]{:S(2)}) collective-permute-start(bf16[4,256,768]{2,0,1:T(4,128)(2,1)} %reshape.713), channel_id=1, source_target_pairs={{0,8},{4,12},{8,0},{12,4},{16,24},{20,28},{24,16},{28,20},{1,9},{5... | collective-permute-start | bytes 4718600 | tf_op jit(solution)/shard_map/ppermute | solution.py:29
  1922.2 118.0 %collective-permute-start.7 = (bf16[4,256,768]{2,0,1:T(4,128)(2,1)}, bf16[4,256,768]{2,0,1:T(4,128)(2,1)}, u32[]{:S(2)}, u32[]{:S(2)}) collective-permute-start(bf16[4,256,768]{2,0,1:T(4,128)(2,1)} %reshape.700), channel_id=1, source_target_pairs={{0,8},{4,12},{8,0},{12,4},{16,24},{20,28},{24,16},{28,20},{1,9},{5... | collective-permute-start | bytes 4718600 | tf_op jit(solution)/shard_map/ppermute | solution.py:29
  1923.2 3.8 collective-permute-start.15
  1927.1 95.1 %collective-permute-start.16 = (s32[4,1024]{1,0:T(4,128)S(1)}, s32[4,1024]{1,0:T(4,128)S(1)}, u32[]{:S(2)}, u32[]{:S(2)}) collective-permute-start(s32[4,1024]{1,0:T(4,128)S(1)} %reshape.718), channel_id=1, source_target_pairs={{0,8},{4,12},{8,0},{12,4},{16,24},{20,28},{24,16},{28,20},{1,9},{5... | collective-permute-start | bytes 49160 | tf_op jit(solution)/shard_map/ppermute | solution.py:29
  2022.3 16.9 collective-permute-start.17
  2039.2 161.2 %collective-permute-start.14 = (bf16[4,256,768]{2,0,1:T(4,128)(2,1)}, bf16[4,256,768]{2,0,1:T(4,128)(2,1)}, u32[]{:S(2)}, u32[]{:S(2)}) collective-permute-start(bf16[4,256,768]{2,0,1:T(4,128)(2,1)} %dynamic-slice_bitcast_fusion.1), channel_id=1, source_target_pairs={{0,16},{4,20},{8,24},{12,28},{16,0},{20,4},{24,8},{28,12},{1,17},{... | collective-permute-start | bytes 4718600 | tf_op jit(solution)/shard_map/ppermute | solution.py:29
  2053.2 157.0 %collective-permute-start.8 = (bf16[4,256,768]{2,0,1:T(4,128)(2,1)}, bf16[4,256,768]{2,0,1:T(4,128)(2,1)}, u32[]{:S(2)}, u32[]{:S(2)}) collective-permute-start(bf16[4,256,768]{2,0,1:T(4,128)(2,1)} %dynamic-slice_bitcast_fusion.3), channel_id=1, source_target_pairs={{0,16},{4,20},{8,24},{12,28},{16,0},{20,4},{24,8},{28,12},{1,17},{... | collective-permute-start | bytes 4718600 | tf_op jit(solution)/shard_map/ppermute | solution.py:29
  (117 other events, 1844.1 us)
Sparse Core Ops, SparseCore 0:
  251.0 45.5 all-gather.4
  424.4 220.6 all-reduce.23
  659.0 46.2 all-gather.8
  707.3 82.0 all-gather.6
  882.7 220.6 all-reduce.21
  1300.4 423.8 all-reduce.27
  1731.9 294.5 all-reduce.25
where the time goes:
time: 2270 us; the launch traced here: 2240 us
  waiting for transfers between devices  1060 us (47%)
  local copies, waits for them, and re-layouts  511 us (23%)
  matrix products  264 us (12%)
  blocking collectives  178 us (8%)
  other arithmetic  171 us (8%)
  starting transfers between devices  31 us (1%)
    unnamed x9, waiting for transfers between devices  383 us
    ppermute x18, waiting for transfers between devices, partner(): lax.ppermute(array, axis, [(i, i ^ 1 << bit) for i in range(lax.axis_size...  358 us
    dynamic_update_slice x20, local copies, waits for them, and re-layouts, butterfly(): lax.dynamic_update_index_in_dim(shaped, arriving.reshape(leaving.shape),...  204 us
    psum x1, waiting for transfers between devices, local(): second_norm_gradient = lax.psum(norm_two_part, 'head')  181 us
    psum x1, blocking collectives, local(): lax.psum((grad_ln1_gain, grad_ln1_bias, grad_w_query, grad_b_query, grad_...  124 us
    all_gather x1, waiting for transfers between devices, local(): lax.all_gather(middle_part.reshape(owned_row_count, portion_rows, width),...  71.3 us
    unnamed x3, blocking collectives  54.2 us
  transfers between devices with their start and end apart: 25, of which 15 were waited for; matrix products, arithmetic and copies ran while one was open for 18% of the time, Pallas kernels for 0%

commit v1 on v0

v1 whole, which is shorter than its diff:
```python
import functools
import math

import jax
import jax.numpy as jnp
from jax import lax
from jax.experimental import pallas as pl
from jax.experimental.pallas import tpu as pltpu
from jax.sharding import PartitionSpec as P

HD = 64
CODONS = 64
EPSILON = 1e-05
NEGATIVE = -1e30
PAIR = 2 * HD
LOG2E = 1.4426950408889634
QUERY_SCALE = HD ** (-0.5) * LOG2E
QCHUNK = 256
KCHUNK = 512
FCHUNK = 256
STRIP = 128
CALLS = ((0, 1), (1, 2), (3, 1), (4, 1), (5, 1))
PART_BITS = 2
PARTS = 1 << PART_BITS
UNIT = 16
VECTOR_ROWS = 16
SMALL_ROWS = 16

F32 = jnp.float32
BF16 = jnp.bfloat16
MIB = 1024 * 1024
LIMIT = 60 * MIB


def dot_nn(a, b):
    return lax.dot_general(a, b, (((1,), (0,)), ((), ())), preferred_element_type=F32)


def dot_nt(a, b):
    return lax.dot_general(a, b, (((1,), (1,)), ((), ())), preferred_element_type=F32)


def standardize(rows):
    center = jnp.mean(rows, axis=-1, keepdims=True)
    shifted = rows - center
    inverse = lax.rsqrt(jnp.mean(shifted * shifted, axis=-1, keepdims=True) + EPSILON)
    return shifted * inverse, inverse


def turn(tile, cos, sin):
    lane = lax.broadcasted_iota(jnp.int32, tile.shape, 1)
    swapped = jnp.where(
        lane % HD < HD // 2,
        pltpu.roll(tile, PAIR - HD // 2, 1),
        pltpu.roll(tile, HD // 2, 1),
    )
    return tile * cos + swapped * sin


def split_three(value):
    high = value.astype(BF16).astype(F32)
    rest = value - high
    mid = rest.astype(BF16).astype(F32)
    return high, mid, rest - mid


def aligned(value, multiple):
    return pl.multiple_of(value, multiple)


class RowCopy:
    def __init__(self, piece, target, sems):
        slots, portion, _ = target.shape
        self.copies = [
            pltpu.make_async_copy(
                piece.at[pl.ds(n * portion, portion)], target.at[n], sems.at[n]
            )
            for n in range(slots)
        ]

    def start(self):
        for copy in self.copies:
            copy.start()

    def wait(self):
        for copy in self.copies:
            copy.wait()


def fetch(step, pieces, buffer, sems):
    copies = [
        RowCopy(pieces[k], buffer.at[k % 2], sems.at[k % 2]) for k in range(len(pieces))
    ]

    @pl.when(step == 0)
    def _():
        copies[0].start()

    for k, copy in enumerate(copies):
        @pl.when(step == k - 1)
        def _(copy=copy):
            copy.start()

    for k, copy in enumerate(copies):
        @pl.when(step == k)
        def _(copy=copy):
            copy.wait()


def emit(step, value, targets, buffer, sems):
    copies = [
        pltpu.make_async_copy(buffer.at[k % 2], targets[k], sems.at[k % 2])
        for k in range(len(targets))
    ]
    last = len(copies) - 1
    for k in range(2, len(copies)):
        @pl.when(step == k)
        def _(k=k):
            copies[k - 2].wait()

    buffer[step % 2] = value
    for k, copy in enumerate(copies):
        @pl.when(step == k)
        def _(copy=copy):
            copy.start()

    @pl.when(step == last)
    def _():
        for copy in copies[max(last - 1, 0) :]:
            copy.wait()


def weight_plan(meta, rows):
    here, side = meta[0], meta[1] % 2
    half = rows // 2
    return [
        (0, here, 0, rows),
        (1, here ^ 1, 0, rows),
        (2, here ^ 2, side * half, half),
        (3, here ^ 2, (1 - side) * half, half),
        (4, here ^ 3, side * half, half),
        (5, here ^ 3, (1 - side) * half, half),
    ]


def head_copies(meta, pieces, which, target, sems, base):
    copies = []
    for i, block, offset, size in weight_plan(meta, HEADS_EACH * HD):
        step = size // HEADS_EACH
        for c in range(HEADS_EACH):
            row = offset + c * step
            place = (row // HD * HEAD_DEVICES + block) * HD + row % HD
            copies.append(
                pltpu.make_async_copy(
                    pieces[i].at[pl.ds(SQUARE_FIRST[i] + which * size + c * step, step)],
                    target.at[pl.ds(aligned(place, UNIT), step)],
                    sems.at[base + len(copies)],
                )
            )
    return copies


def block_copies(meta, pieces, which, target, sems, base):
    return [
        pltpu.make_async_copy(
            pieces[i].at[which],
            target.at[block, pl.ds(aligned(offset, UNIT), size)],
            sems.at[base + i],
        )
        for i, block, offset, size in weight_plan(meta, pieces[0].shape[1])
    ]


HEADS_EACH = 3
HEAD_DEVICES = 4
SQUARE_FIRST = (0, 0, 512, 0, 0, 0)
PIECES = 6
HEAD_COPIES = PIECES * HEADS_EACH


def project_kernel(count, meta, *refs):
    toks, weights = refs[:count], refs[count : count + PIECES]
    vec, cos_ref, sin_ref = refs[count + PIECES : count + PIECES + 3]
    n_out, q_out, k_out, v_out, buffer, wq, wk, wv, tok_sems, sems = refs[count + PIECES + 3 :]
    step = pl.program_id(0)
    _, slots, portion, width = buffer.shape
    copies = []
    for i, ref in enumerate((wq, wk, wv)):
        copies += head_copies(meta, weights, i, ref, sems, i * HEAD_COPIES)

    @pl.when(step == 0)
    def _():
        for copy in copies:
            copy.start()

    fetch(step, toks, buffer, tok_sems)
    tok = buffer[step % 2].reshape(slots * portion, width).astype(F32)
    standard, _ = standardize(tok)
    normed = (standard * vec[5:6, :] + vec[6:7, :]).astype(BF16)
    n_out[...] = normed.reshape(slots, portion, width)

    @pl.when(step == 0)
    def _():
        for copy in copies:
            copy.wait()

    cos = jnp.concatenate([cos_ref[...]] * slots, axis=0)
    sin = jnp.concatenate([sin_ref[...]] * slots, axis=0)
    query = dot_nt(normed, wq[...]) + vec[0:1, :]
    key = dot_nt(normed, wk[...]) + vec[1:2, :]
    for j in range(width // PAIR):
        at = slice(j * PAIR, (j + 1) * PAIR)
        q_out[:, :, at] = (
            (turn(query[:, at], cos, sin) * QUERY_SCALE)
            .astype(BF16)
            .reshape(slots, portion, PAIR)
        )
        k_out[:, :, at] = (
            turn(key[:, at], cos, sin).astype(BF16).reshape(slots, portion, PAIR)
        )
    value = dot_nt(normed, wv[...]) + vec[2:3, :]
    v_out[...] = value.astype(BF16).reshape(slots, portion, width)


def attend_kernel(slot, meta, q_ref, k_ref, v_ref, *refs):
    o_ref, rest_ref, st_ref = refs[-3:]
    length = meta[2 + slot]
    rows = k_ref.shape[1]
    lane = lax.broadcasted_iota(jnp.int32, (rows, PAIR), 1)
    place_in = lax.broadcasted_iota(jnp.int32, (rows, PAIR), 0)
    halves = [(lane // HD == h).astype(F32).astype(BF16) for h in range(2)]
    guard = jnp.where(
        lane % HD == 3, jnp.where(place_in < length, 0.0, NEGATIVE), 1.0
    ).astype(BF16)
    keys = jnp.concatenate([k_ref[0], guard], axis=1)
    values = v_ref[0]
    values_h = [values * half + (1.0 - half) for half in halves]
    short = (QCHUNK, PAIR)
    lane_c = lax.broadcasted_iota(jnp.int32, short, 1)
    first = lane_c < HD
    within = lane_c % HD
    flag = (lane_c == 3).astype(F32).astype(BF16)

    def scores_of(i):
        c, h = divmod(i, 2)
        at = slice(c * QCHUNK, (c + 1) * QCHUNK)
        query = jnp.concatenate([q_ref[0, at, :] * halves[h][:QCHUNK], flag], axis=1)
        return dot_nt(query, keys)

    steps = 2 * (rows // QCHUNK)
    following = scores_of(0)
    outs, logs = [], []
    for i in range(steps):
        c, h = divmod(i, 2)
        scores = following
        if i + 1 < steps:
            following = scores_of(i + 1)
        top = jnp.max(scores, axis=1, keepdims=True)
        weights = jnp.exp2(scores - top).astype(BF16)
        sums = dot_nn(weights, values_h[h])
        total = pltpu.roll(sums, HD, 1)
        outs.append(sums / total)
        logs.append(-top - jnp.log(total) * LOG2E)
        if h == 1:
            at = slice(c * QCHUNK, (c + 1) * QCHUNK)
            context = jnp.where(first, outs[0], outs[1])
            o_ref[0, at, :] = context.astype(BF16)
            rest_ref[0, at, :] = (context - context.astype(BF16).astype(F32)).astype(BF16)
            high, mid, low = split_three(jnp.where(first, logs[0], logs[1]))
            st_ref[0, at, :] = jnp.where(
                within == 0,
                high,
                jnp.where(
                    within == 1,
                    mid,
                    jnp.where(within == 2, low, jnp.where(within == 3, 1.0, 0.0)),
                ),
            ).astype(BF16)
            outs, logs = [], []


def attend_back_kernel(
    meta,
    q_ref,
    k_ref,
    v_ref,
    do_ref,
    o_ref,
    rest_ref,
    st_ref,
    cos_ref,
    sin_ref,
    dq_ref,
    dk_ref,
    dv_ref,
    sums_ref,
    dqt,
):
    length = meta[2 + pl.program_id(0)]
    rows = k_ref.shape[1]
    lane = lax.broadcasted_iota(jnp.int32, (rows, PAIR), 1)
    within = lane % HD
    place_in = lax.broadcasted_iota(jnp.int32, (rows, PAIR), 0)
    halves = [(lane // HD == h).astype(F32).astype(BF16) for h in range(2)]
    guard = jnp.where(within == 3, jnp.where(place_in < length, 0.0, NEGATIVE), 1.0).astype(BF16)
    key = k_ref[0]
    keys = jnp.concatenate([key, guard], axis=1)
    values = jnp.concatenate([v_ref[0], jnp.ones((rows, PAIR), BF16)], axis=1)
    grads = do_ref[0]
    product = grads.astype(F32) * (o_ref[0].astype(F32) + rest_ref[0].astype(F32))
    p_high = product.astype(BF16)
    p_low = (product - p_high.astype(F32)).astype(BF16)
    ones_row = lax.broadcasted_iota(jnp.int32, (PAIR, PAIR), 0) // HD
    ones_col = lax.broadcasted_iota(jnp.int32, (PAIR, PAIR), 1) // HD
    blocks = (ones_row == ones_col).astype(F32).astype(BF16)
    high, mid, low = split_three(-(dot_nn(p_high, blocks) + dot_nn(p_low, blocks)))
    offsets = jnp.where(
        within == 0, high, jnp.where(within == 1, mid, jnp.where(within == 2, low, 0.0))
    ).astype(BF16)
    stats = st_ref[0]
    query = q_ref[0]
    query_h = [query * half for half in halves]
    grads_h = [grads * half for half in halves]
    query_x = [jnp.concatenate([query_h[h], stats * halves[h]], axis=1) for h in range(2)]
    grads_x = [jnp.concatenate([grads_h[h], offsets * halves[h]], axis=1) for h in range(2)]
    key_t = key.T
    key_sum = jnp.zeros((1, PAIR), F32)
    value_sum = jnp.zeros((1, PAIR), F32)

    def products(i):
        c, h = divmod(i, 2)
        at = slice(c * KCHUNK, (c + 1) * KCHUNK)
        return dot_nt(keys[at], query_x[h]), dot_nt(values[at], grads_x[h])

    steps = 2 * (rows // KCHUNK)
    following = products(0)
    for i in range(steps):
        c, h = divmod(i, 2)
        at = slice(c * KCHUNK, (c + 1) * KCHUNK)
        scores, weight_grad = following
        if i + 1 < steps:
            following = products(i + 1)
        if h == 0:
            value_grad = jnp.zeros((KCHUNK, PAIR), F32)
            key_grad = jnp.zeros((KCHUNK, PAIR), F32)
        weights = jnp.exp2(scores)
        score_grad = (weights * weight_grad).astype(BF16)
        value_grad += dot_nn(weights.astype(BF16), grads_h[h])
        key_grad += dot_nn(score_grad, query_h[h])
        head = slice(h * HD, (h + 1) * HD)
        part = dot_nn(key_t[head, at], score_grad)
        if c == 0:
            dqt[head, :] = part
        else:
            dqt[head, :] += part
        if h == 1:
            key_grad = turn(key_grad * (1.0 / LOG2E), cos_ref[at, :], -sin_ref[at, :])
            dv_ref[0, at, :] = value_grad.astype(BF16)
            dk_ref[0, at, :] = key_grad.astype(BF16)
            value_sum += jnp.sum(value_grad, axis=0, keepdims=True)
            key_sum += jnp.sum(key_grad, axis=0, keepdims=True)
    query_grad = turn(dqt[...].T * (HD ** (-0.5)), cos_ref[...], -sin_ref[...])
    dq_ref[0] = query_grad.astype(BF16)
    sums_ref[0, 0:1, :] = jnp.sum(query_grad, axis=0, keepdims=True)
    sums_ref[0, 1:2, :] = key_sum
    sums_ref[0, 2:3, :] = value_sum


def gelu_parts(pre):
    magnitude = jnp.abs(pre)
    bell = jnp.exp2(pre * pre * (-0.5 * LOG2E))
    divisor = 1.0 + (0.3275911 / math.sqrt(2.0)) * magnitude
    t = pl.reciprocal(divisor, approx=True)
    t = t * (2.0 - divisor * t)
    poly = t * (
        0.5 * 0.254829592
        + t
        * (
            0.5 * -0.284496736
            + t * (0.5 * 1.421413741 + t * (0.5 * -1.453152027 + t * (0.5 * 1.061405429)))
        )
    )
    tail = poly * bell
    share = jnp.where(pre > 0.0, 1.0 - tail, tail)
    return pre * share, share + pre * bell * (1.0 / math.sqrt(2.0 * math.pi))


SIDE_ORDER = ("side", "s0", "s1")
SEQ_ORDER = ("s0", "s1", "side")


def scatter_plan(order):
    plan = []
    names = ("core", "side", "s0", "s1")
    for number in range(1 << len(names)):
        bits = {name: number >> i & 1 for i, name in enumerate(names)}
        slot = 0
        for name in order:
            slot = slot * 2 + bits[name]
        plan.append((bits["core"] + 2 * bits["side"], bits["s0"] + 2 * bits["s1"], bits["core"], slot))
    return plan


def feed_kernel(count, orders, meta, *refs):
    toks, cots, refs = refs[:count], refs[count : 2 * count], refs[2 * count :]
    square_pieces, refs = refs[:PIECES], refs[PIECES:]
    block_pieces, refs = refs[:PIECES], refs[PIECES:]
    ctx, vec, b_up, refs = refs[0], refs[1], refs[2], refs[3:]
    mixed_refs, refs = refs[:count], refs[count:]
    mg_ref, dctx_ref, vec_ref, up_stay, up_leave, down_stay, down_leave = refs[:7]
    (
        tok_buf,
        cot_buf,
        mix_buf,
        w_out,
        w_up,
        w_down,
        hid,
        slope,
        dup,
        ddown,
        dout,
        standard,
        acc,
        normed,
        normed_t,
        grad_low,
        grad_t,
        ctx_t,
        inverse,
        tok_sems,
        cot_sems,
        mix_sems,
        w_sems,
        sems,
    ) = refs[7:]
    step = pl.program_id(0)
    _, slots, portion, width = tok_buf.shape
    groups = w_up.shape[0]
    total_rows = slots * portion
    chunks = [slice(f, f + FCHUNK) for f in range(0, width, FCHUNK)]
    first_row = (step ^ meta[0]) * portion
    early = head_copies(meta, square_pieces, 3, w_out, w_sems, 0)
    late = block_copies(meta, block_pieces, 0, w_up, w_sems, HEAD_COPIES)
    late += block_copies(meta, block_pieces, 1, w_down, w_sems, HEAD_COPIES + PIECES)

    @pl.when(step == 0)
    def _():
        for copy in early + late:
            copy.start()

    fetch(step, toks, tok_buf, tok_sems)
    fetch(step, cots, cot_buf, cot_sems)

    def mix_copy(k):
        return pltpu.make_async_copy(mix_buf.at[0], mixed_refs[k], mix_sems.at[k % 2])

    @pl.when(step == 0)
    def _():
        for ref in (dup, ddown, dout, vec_ref, hid, grad_t):
            ref[...] = jnp.zeros_like(ref)
        for copy in early + late:
            copy.wait()

    for k in range(1, count):
        @pl.when(step == k)
        def _(k=k):
            mix_copy(k - 1).wait()

    spots = [(j, at) for j in range(groups) for at in chunks]
    per = len(chunks)
    parity = step % 2
    strips = []
    for n in range(slots):
        for inner in range(0, portion, STRIP):
            index = lax.broadcasted_iota(jnp.int32, (STRIP, 1), 0) + first_row + inner
            first = n * portion + inner
            strips.append(
                (slice(first, first + STRIP), n, slice(inner, inner + STRIP), index < meta[2 + n])
            )
    assert len(strips) == groups and len(spots) == 3 * groups

    def normalize(at, slot, inner, alive):
        middle = tok_buf[parity, slot, inner, :].astype(F32) + acc[at, :] + vec[3:4, :]
        std, inv = standardize(middle)
        standard[at, :] = std
        inverse[at, :] = jnp.broadcast_to(inv, (STRIP, PAIR))
        acc[at, :] = middle + vec[4:5, :]
        normed[at, :] = (std * vec[7:8, :] + vec[8:9, :]).astype(BF16)

    def take_grad(at, slot, inner, alive):
        out_grad = jnp.where(alive, cot_buf[parity, slot, inner, :].astype(F32), 0.0)
        vec_ref[4:5, :] += jnp.sum(out_grad, axis=0, keepdims=True)
        grad_low[at, :] = out_grad.astype(BF16)
        normed_t[:, at] = normed[at, :].T

    def finish(at, slot, inner, alive):
        mix_buf[0, slot, inner, :] = jnp.where(alive, acc[at, :], 0.0).astype(BF16)

    def denormalize(at, slot, inner, alive):
        norm_grad, std = acc[at, :], standard[at, :]
        vec_ref[7:8, :] += jnp.sum(norm_grad * std, axis=0, keepdims=True)
        vec_ref[8:9, :] += jnp.sum(norm_grad, axis=0, keepdims=True)
        scaled = norm_grad * vec[7:8, :]
        middle_grad = grad_low[at, :].astype(F32) + inverse[at, 0:1] * (
            scaled
            - jnp.mean(scaled, axis=-1, keepdims=True)
            - std * jnp.mean(scaled * std, axis=-1, keepdims=True)
        )
        vec_ref[3:4, :] += jnp.sum(middle_grad, axis=0, keepdims=True)
        mg_ref[slot, inner, :] = middle_grad.astype(BF16)

    def up_dot(i):
        j, at = spots[i]
        return dot_nn(normed[...], w_up[j, :, at])

    def hidden_dot(i):
        j, at = spots[i]
        return dot_nt(grad_low[...], w_down[j, at, :])

    acc[...] = dot_nn(ctx[...].reshape(total_rows, width), w_out[...])
    for s, strip in enumerate(strips):
        normalize(*strip)
        ddown[s] += dot_nn(grad_t[...], hid[s])

    following = up_dot(0)
    for i, (j, at) in enumerate(spots):
        pre = following + b_up[j, :, at]
        if i + 1 < len(spots):
            following = up_dot(i + 1)
        if i % per == per - 1 and j > 0:
            acc[...] += dot_nn(hid[j - 1], w_down[j - 1])
        rows_at, slot, inner, _ = strips[i % groups]
        if i < groups:
            take_grad(*strips[i])
        elif i < 2 * groups:
            grad_t[:, rows_at] = grad_low[rows_at, :].T
        else:
            ctx_t[:, rows_at] = ctx[slot, inner, :].T
        hidden, bend = gelu_parts(pre)
        hid[j, :, at] = hidden.astype(BF16)
        slope[j, :, at] = bend.astype(BF16)

    following = hidden_dot(0)
    acc[...] += dot_nn(hid[groups - 1], w_down[groups - 1])
    for i, (j, at) in enumerate(spots):
        back = following
        if i + 1 < len(spots):
            following = hidden_dot(i + 1)
        if i < groups // 2:
            finish(*strips[2 * i])
            finish(*strips[2 * i + 1])
        if i % per == 0 and j > 0:
            part = dot_nt(slope[j - 1], w_up[j - 1])
            if j == 1:
                acc[...] = part
            else:
                acc[...] += part
        pre_grad = back * slope[j, :, at].astype(F32)
        vec_ref[9 + j : 10 + j, at] += jnp.sum(pre_grad, axis=0, keepdims=True)
        slope[j, :, at] = pre_grad.astype(BF16)
    acc[...] += dot_nt(slope[groups - 1], w_up[groups - 1])

    def turn_back(s, carry):
        per_slot = portion // STRIP
        at = pl.ds(aligned(s * STRIP, STRIP), STRIP)
        denormalize(at, s // per_slot, pl.ds(aligned(s % per_slot * STRIP, STRIP), STRIP), None)
        dup[s] += dot_nn(normed_t[...], slope[s])
        return carry

    lax.fori_loop(0, groups, turn_back, 0)
    middle_low = mg_ref[...].reshape(total_rows, width)
    dctx_ref[...] = dot_nt(middle_low, w_out[...]).astype(BF16).reshape(slots, portion, width)
    dout[...] += dot_nn(ctx_t[...], middle_low)
    for k in range(count):
        @pl.when(step == k)
        def _(k=k):
            mix_copy(k).start()

    @pl.when(step == pl.num_programs(0) - 1)
    def _():
        mix_copy(count - 1).wait()

        def last_share(j, carry):
            ddown[j] += dot_nn(grad_t[...], hid[j])
            return carry

        lax.fori_loop(0, groups, last_share, 0)

    @pl.when(step == pl.num_programs(0) - 1)
    def _():
        here, position = meta[0], meta[1] % PARTS
        size = width // PARTS
        per_block = hid.shape[1] // size
        ring = hid.shape[0] * per_block
        o_size = HEADS_EACH * UNIT
        o_per_block = slope.shape[1] // o_size
        copies, o_copies = [], []
        for source, order, stay, leave in (
            (dup, orders[0], up_stay, up_leave),
            (ddown, orders[1], down_stay, down_leave),
        ):
            for block, part, away, slot in scatter_plan(order):
                number = len(copies) % ring
                if len(copies) >= ring:
                    copies[-ring].wait()
                stage = hid.at[number // per_block, pl.ds(number % per_block * size, size)]
                first = aligned((part ^ position) * size, size)
                stage[...] = source[here ^ block, pl.ds(first, size), :].astype(BF16)
                target = leave if away else stay
                copies.append(
                    pltpu.make_async_copy(stage, target.at[slot, pl.ds(0, size)], sems.at[number])
                )
                copies[-1].start()
                if source is dup:
                    continue
                number = len(o_copies)
                stage = slope.at[
                    number // o_per_block, pl.ds(number % o_per_block * o_size, o_size)
                ]
                for i in range(HEADS_EACH):
                    first = (i * HEAD_DEVICES + (here ^ block)) * HD + (part ^ position) * UNIT
                    stage[i * UNIT : (i + 1) * UNIT, :] = dout[
                        pl.ds(aligned(first, UNIT), UNIT), :
                    ].astype(BF16)
                o_copies.append(
                    pltpu.make_async_copy(
                        stage, target.at[slot, pl.ds(size, o_size)], sems.at[ring + number]
                    )
                )
                o_copies[-1].start()
        for copy in copies[-ring:] + o_copies:
            copy.wait()


def weight_kernel(columns, heads, meta, *refs):
    grads, refs = refs[: 3 * columns], refs[3 * columns :]
    normed, outs, acc = refs[0], refs[1:-1], refs[-1]
    step = pl.program_id(0)
    total_rows = normed.shape[0] * normed.shape[1]
    width = normed.shape[2]

    @pl.when(step == 0)
    def _():
        acc[...] = jnp.zeros_like(acc)

    turned = [
        grads[3 * p + i][...].reshape(total_rows, grads[3 * p + i].shape[-1]).T
        for i in range(3)
        for p in range(columns)
    ]
    acc[...] += dot_nn(jnp.concatenate(turned, axis=0), normed[...].reshape(total_rows, width))

    @pl.when(step == pl.num_programs(0) - 1)
    def _():
        here, side = meta[0], meta[1] % 2
        unit = HD // 2
        for block, out in enumerate(outs):
            for part in range(2):
                for i in range(3):
                    for head in range(heads):
                        first = ((i * heads + head) * HEAD_DEVICES + (here ^ block)) * HD
                        first = aligned(first + (part ^ side) * unit, unit)
                        place = (i * heads + head) * unit
                        out[part, place : place + unit, :] = acc[pl.ds(first, unit), :].astype(
                            BF16
                        )


def vectors_kernel(count, meta, *refs):
    pieces, (vec, bias_up, buffer, sems) = refs[:count], refs[count:]
    copies = [
        pltpu.make_async_copy(
            ref.at[pl.ds(ref.shape[0] - SMALL_ROWS, SMALL_ROWS)], buffer.at[k], sems.at[k]
        )
        for k, ref in enumerate(pieces)
    ]
    for copy in copies:
        copy.start()
    for copy in copies:
        copy.wait()
    values = [buffer[k].astype(F32) for k in range(count)]
    part = HEADS_EACH * HD
    vec[...] = jnp.zeros_like(vec)
    for g in range(count):
        at = meta[0] ^ g
        mine = values[0]
        for k in range(1, count):
            mine = jnp.where(at == k, values[k], mine)
        for i in range(13):
            row = mine[i // 4 : i // 4 + 1, i % 4 * part : (i % 4 + 1) * part]
            if i < 3:
                for head in range(HEADS_EACH):
                    place = (head * count + g) * HD
                    vec[i : i + 1, place : place + HD] = row[:, head * HD : (head + 1) * HD]
            elif i < 9:
                vec[i : i + 1, g * part : (g + 1) * part] = row
            else:
                bias_up[g, :, (i - 9) * part : (i - 8) * part] = row


def input_kernel(count, columns, opening, meta, *refs):
    toks, weights = refs[:count], refs[count : count + PIECES]
    refs = refs[count + PIECES :]
    grads, refs = refs[: 4 * columns], refs[4 * columns :]
    vec, vec_in, mg = refs[:3]
    out_refs, refs = refs[3 : 3 + count], refs[3 + count :]
    vec_ref, buffer, out_buf, wq, wk, wv, tok_sems, out_sems, w_sems = refs
    step = pl.program_id(0)
    _, slots, portion, width = buffer.shape
    total_rows = slots * portion
    copies = []
    for i, ref in enumerate((wq, wk, wv)):
        copies += head_copies(meta, weights, i, ref, w_sems, i * HEAD_COPIES)

    @pl.when(step == 0)
    def _():
        for copy in copies:
            copy.start()

    fetch(step, toks, buffer, tok_sems)

    @pl.when(step == 0)
    def _():
        vec_ref[...] = vec_in[...]
        if opening:
            for i in range(3):
                vec_ref[i : i + 1, :] = jnp.concatenate(
                    [
                        jnp.sum(grads[4 * p + 3][:, i, :], axis=0, keepdims=True)
                        for p in range(columns)
                    ],
                    axis=1,
                )
        for copy in copies:
            copy.wait()

    tok = buffer[step % 2].reshape(total_rows, width).astype(F32)
    standard, inverse = standardize(tok)
    norm_grad = jnp.zeros((total_rows, width), F32)
    for i, weight in enumerate((wq, wk, wv)):
        low = jnp.concatenate(
            [
                grads[4 * p + i][...].reshape(total_rows, grads[4 * p + i].shape[-1])
                for p in range(columns)
            ],
            axis=1,
        )
        norm_grad += dot_nn(low, weight[...])
    vec_ref[5:6, :] += jnp.sum(norm_grad * standard, axis=0, keepdims=True)
    vec_ref[6:7, :] += jnp.sum(norm_grad, axis=0, keepdims=True)
    scaled = norm_grad * vec[5:6, :]
    result = mg[...].reshape(total_rows, width).astype(F32) + inverse * (
        scaled
        - jnp.mean(scaled, axis=-1, keepdims=True)
        - standard * jnp.mean(scaled * standard, axis=-1, keepdims=True)
    )
    emit(step, result.astype(BF16).reshape(slots, portion, width), out_refs, out_buf, out_sems)


def rest_units(first_bits, inputs, position):
    near, far = inputs
    one, two = first_bits
    for number in range(PARTS):
        yield (
            number ^ position,
            far if number >> two & 1 else near,
            number >> one & 1,
        )


def unpack_up_kernel(first_bits, meta, near, far, out):
    size = out.shape[0] // PARTS
    for part, ref, index in rest_units(first_bits, (near, far), meta[1] % PARTS):
        out[pl.ds(aligned(part * size, 8), size), :] = ref[index].astype(F32)


def unpack_down_kernel(first_bits, meta, near, far, down, out, scratch):
    size = down.shape[0] // PARTS
    for part, ref, index in rest_units(first_bits, (near, far), meta[1] % PARTS):
        scratch[pl.ds(aligned(part * size, 8), size), :] = ref[index, :size, :].astype(F32)
        for i in range(HEADS_EACH):
            first = aligned(i * HD + part * UNIT, 8)
            unit = size + i * UNIT
            out[pl.ds(first, UNIT), :] = ref[index, unit : unit + UNIT, :].astype(F32)
    down[...] = scratch[...].T


def unpack_heads_kernel(early_heads, meta, near, far, near_late, far_late, *outs):
    unit = HD // 2
    for inputs, heads in (
        ((near, far), range(early_heads)),
        ((near_late, far_late), range(early_heads, HEADS_EACH)),
    ):
        for number, ref in enumerate(inputs):
            part = number ^ (meta[1] % 2)
            for i, out in enumerate(outs):
                for place, head in enumerate(heads):
                    first = aligned(head * HD + part * unit, 8)
                    at = (i * len(heads) + place) * unit
                    out[pl.ds(first, unit), :] = ref[0, at : at + unit, :].astype(F32)


def place_kernel(count, meta, *refs):
    out = refs[count]
    for k in range(count):
        out[:, meta[0] ^ k] = refs[k][...]


def whole(shape):
    return pl.BlockSpec(
        shape, lambda *_: (0,) * len(shape), pipeline_mode=pl.Buffered(buffer_count=1)
    )


ANYWHERE = pl.BlockSpec(memory_space=pl.ANY)


def call(kernel, name, meta, args, grid, in_specs, out_specs, out_shape, scratch=(), cost=None, aliases=None):
    return pl.pallas_call(
        kernel,
        grid_spec=pltpu.PrefetchScalarGridSpec(
            num_scalar_prefetch=1,
            grid=grid,
            in_specs=in_specs,
            out_specs=out_specs,
            scratch_shapes=list(scratch),
        ),
        out_shape=out_shape,
        compiler_params=pltpu.CompilerParams(vmem_limit_bytes=LIMIT),
        cost_estimate=pl.CostEstimate(flops=1, bytes_accessed=1, transcendentals=0),
        input_output_aliases=aliases or {},
        name=name,
    )(meta, *args)


def local(
    tokens,
    cotangent,
    lengths,
    owners,
    codons,
    ln1_gain,
    ln1_bias,
    w_query,
    b_query,
    w_key,
    b_key,
    w_value,
    b_value,
    w_out,
    b_out,
    ln2_gain,
    ln2_bias,
    w_up,
    b_up,
    w_down,
    b_down,
):
    heads = lax.axis_size("head")
    peers = lax.axis_size("seq")
    here = lax.axis_index("head").astype(jnp.int32)
    position = lax.axis_index("seq").astype(jnp.int32)
    total_slots, portion, width = tokens.shape
    slots = total_slots // heads
    rows = portion * heads
    part_width = ln1_gain.shape[0]
    assert heads == HEAD_DEVICES and part_width == HEADS_EACH * HD
    assert peers >= PARTS and peers & peers - 1 == 0
    peer_bits = peers.bit_length() - 1

    def tie(*values):
        return lax.optimization_barrier(values)

    def swap(array, bits, axis="head"):
        size = lax.axis_size(axis)
        return lax.ppermute(array, axis, [(i, i ^ bits) for i in range(size)])

    def move(array, name):
        if name == "core":
            return swap(array, 1)
        if name == "side":
            return swap(array, 2)
        return swap(array, 1 << int(name[1:]), "seq")

    def add(one, other):
        return (one.astype(F32) + other.astype(F32)).astype(BF16)


    def row_slices(array):
        view = array.reshape(slots, heads, portion, width)
        return [
            lax.dynamic_index_in_dim(view, here ^ k, 1, keepdims=False).reshape(
                slots * portion, width
            )
            for k in range(heads)
        ]

    def send_rows(pieces):
        moved = {k: swap(pieces[k], k) for k in (2, 3, 1)}
        return [pieces[0]] + [moved[k] for k in range(1, heads)]

    def gather(shard):
        half = shard.shape[1] // 2
        mine = lax.dynamic_slice_in_dim(shard, position % 2 * half, half, 1)
        across = swap(mine, 2)
        beside = swap(across, 1, "seq")
        return [shard, swap(shard, 1), across, beside, swap(across, 1), swap(beside, 1)]

    named = 9
    packed = jnp.concatenate(
        [b_query, b_key, b_value, b_out, b_down, ln1_gain, ln1_bias, ln2_gain, ln2_bias, b_up]
        + [jnp.zeros((SMALL_ROWS * width - (named + heads) * part_width,), BF16)]
    ).reshape(SMALL_ROWS, width)
    token_slices = row_slices(tokens)
    square_parts = [w_query, w_key, w_value, w_out]
    square = jnp.concatenate(square_parts + [packed], axis=0)
    half_width = part_width // 2
    assert slots * portion == SQUARE_FIRST[2]
    first_load = jnp.concatenate(
        [token_slices[2]]
        + [
            lax.dynamic_slice_in_dim(part, position % 2 * half_width, half_width, 0)
            for part in square_parts
        ]
        + [packed],
        axis=0,
    )
    first_load, token_slices, square = tie(first_load, token_slices, square)
    first_across = swap(first_load, 2)
    tok_core = swap(token_slices[1], 1)
    square_core = swap(square, 1)
    first_across, tok_core, square_core = tie(first_across, tok_core, square_core)
    tok_far = swap(token_slices[3], 3)
    square_across = first_across[SQUARE_FIRST[2] :]
    square_beside = swap(square_across, 1, "seq")
    square_far = swap(square_across, 1)
    block = jnp.stack([w_up, w_down])
    block_half = lax.dynamic_slice_in_dim(block, position % 2 * (width // 2), width // 2, 1)
    square_beside, block, block_half, tok_far, square_far = tie(
        square_beside, block, block_half, tok_far, square_far
    )
    square_last = swap(square_beside, 1)
    block_across = swap(block_half, 2)
    block_core = swap(block, 1)
    cots = send_rows(row_slices(tie(cotangent, square_beside)[0]))
    squares = [square, square_core, first_across, square_beside, square_far, square_last]
    toks = [token_slices[0], tok_core, first_across, tok_far]

    own_lengths = lax.dynamic_index_in_dim(
        lengths.reshape(slots, heads), here, 1, keepdims=False
    ).astype(jnp.int32)
    meta = jnp.concatenate([here.reshape(1), position.reshape(1), own_lengths])

    vec, bias_up = call(
        functools.partial(vectors_kernel, heads),
        "vectors",
        meta,
        [squares[0], squares[1], squares[2], squares[4]],
        (1,),
        [ANYWHERE] * heads,
        [whole((VECTOR_ROWS, width)), whole((heads, 1, width))],
        [
            jax.ShapeDtypeStruct((VECTOR_ROWS, width), F32),
            jax.ShapeDtypeStruct((heads, 1, width), F32),
        ],
        [
            pltpu.VMEM((heads, SMALL_ROWS, width), BF16),
            pltpu.SemaphoreType.DMA((heads,)),
        ],
        cost=(0, 65536),
    )

    half = HD // 2
    frequency = 10000.0 ** (-(jnp.arange(half, dtype=F32) * 2.0 / HD))
    angles = jnp.arange(rows, dtype=F32)[:, None] * frequency[None, :]
    cos, sin = jnp.cos(angles), jnp.sin(angles)
    cos = jnp.concatenate([cos, cos, cos, cos], axis=1)
    sin = jnp.concatenate([-sin, sin, -sin, sin], axis=1)

    low = jax.ShapeDtypeStruct((slots, rows, width), BF16)
    piece = jax.ShapeDtypeStruct((slots, portion, width), BF16)
    vector = jax.ShapeDtypeStruct((VECTOR_ROWS, width), F32)
    work = slots * rows * width
    flat = pl.BlockSpec((slots, portion, width), lambda k, m: (0, k ^ m[0], 0))
    table = pl.BlockSpec((portion, PAIR), lambda k, m: (k ^ m[0], 0))
    square_buffer = pltpu.VMEM((width, width), BF16)
    pair_buffer = pltpu.VMEM((2, slots, portion, width), BF16)
    two = pltpu.SemaphoreType.DMA((2,))
    row_sems = pltpu.SemaphoreType.DMA((2, slots))
    three_heads = pltpu.SemaphoreType.DMA((3 * HEAD_COPIES,))
    vec_spec = whole((VECTOR_ROWS, width))
    vec_out = pl.BlockSpec((VECTOR_ROWS, width), lambda *_: (0, 0))

    normed, q, k, v = call(
        functools.partial(project_kernel, heads),
        "project",
        meta,
        [*toks, *squares, vec, cos, sin],
        (heads,),
        [ANYWHERE] * (heads + PIECES) + [vec_spec, table, table],
        [flat] * 4,
        [low] * 4,
        [pair_buffer, square_buffer, square_buffer, square_buffer, row_sems, three_heads],
        cost=(6 * work * width, 8 * work),
    )

    pairs = width // PAIR
    tile = pl.BlockSpec((1, rows, PAIR), lambda n, p, *_: (n, 0, p))

    def attend(meta, slot, before):
        picked = pl.BlockSpec((1, rows, PAIR), lambda p, *_: (slot, 0, p))
        return call(
            functools.partial(attend_kernel, slot),
            "attend",
            meta,
            [q, k, v, *before],
            (pairs,),
            [picked] * 3 + [ANYWHERE] * len(before),
            [picked] * 3,
            [low] * 3,
            cost=(16 * work * rows // slots, 10 * work // slots),
            aliases={4 + i: i for i in range(len(before))},
        )

    attended = []
    now = meta
    for slot in range(slots):
        if slot == 0:
            now, q, block_across = tie(now, q, block_across)
            block_beside = swap(block_across, 1, "seq")
            block_far = swap(block_across, 1)
        elif slot == 1:
            now, block_beside, attended, cots[2] = tie(meta, block_beside, attended, cots[2])
            blocks = [block, block_core, block_across, block_beside, block_far]
            blocks += [swap(block_beside, 1)]
        attended = attend(now, slot, attended)
    context, context_rest, stats = attended

    size = width // PARTS
    o_size = HEADS_EACH * UNIT
    up_shape = jax.ShapeDtypeStruct((2 * PARTS, size, width), BF16)
    down_shape = jax.ShapeDtypeStruct((2 * PARTS, size + o_size, width), BF16)
    ring = heads * (slots * portion // size)
    block_buffer = pltpu.VMEM((heads, width, width), BF16)
    block_sums = pltpu.VMEM((heads, width, width), F32)
    hidden_buffer = pltpu.VMEM((heads, slots * portion, width), BF16)
    row_sums = pltpu.VMEM((slots * portion, width), F32)
    row_buffer = pltpu.VMEM((slots * portion, width), BF16)
    turned_buffer = pltpu.VMEM((width, slots * portion), BF16)
    out = call(
        functools.partial(feed_kernel, heads, (SIDE_ORDER, SEQ_ORDER)),
        "feed",
        meta,
        [*toks, *cots, *squares, *blocks, context, vec, bias_up],
        (heads,),
        [ANYWHERE] * (2 * heads + 2 * PIECES) + [flat, vec_spec, whole((heads, 1, width))],
        [ANYWHERE] * heads + [flat, flat, vec_out] + [ANYWHERE] * 4,
        [piece] * heads + [low, low, vector] + [up_shape] * 2 + [down_shape] * 2,
        [
            pair_buffer,
            pair_buffer,
            pltpu.VMEM((1, slots, portion, width), BF16),
            square_buffer,
            block_buffer,
            block_buffer,
            hidden_buffer,
            hidden_buffer,
            block_sums,
            block_sums,
            pltpu.VMEM((width, width), F32),
            row_sums,
            row_sums,
            row_buffer,
            turned_buffer,
            row_buffer,
            turned_buffer,
            turned_buffer,
            pltpu.VMEM((slots * portion, PAIR), F32),
            row_sems,
            row_sems,
            two,
            pltpu.SemaphoreType.DMA((HEAD_COPIES + 2 * PIECES,)),
            pltpu.SemaphoreType.DMA((ring + 4 * PARTS,)),
        ],
        cost=(54 * work * width, 60 * MIB),
    )
    mixed, out = out[:heads], out[heads:]
    middle_grad, context_grad, feed_vec, up_stay, up_leave, down_stay, down_leave = out


    class Chain:
        def __init__(self, stay, leave, order, back):
            self.state = (stay, leave)
            self.stages = [("half", "core")] + [("half", name) for name in order]
            self.stages += [("full", f"s{bit}") for bit in range(PART_BITS, peer_bits)]
            self.stages += [("back", name) for name in back]
            self.done = 0
            self.first_bits = tuple(int(name[1:]) for name in back)

        @property
        def open(self):
            return self.done < len(self.stages)

        def start(self):
            self.got = move(self.state[1], self.stages[self.done][1])

        def absorb(self):
            kind = self.stages[self.done][0]
            self.done += 1
            if not self.open:
                self.ends = [self.state[0], self.got]
                return
            if kind == "back":
                current = jnp.concatenate([self.state[0], self.got], axis=0)
            else:
                current = add(self.state[0], self.got)
            if self.stages[self.done][0] == "half":
                count = current.shape[0] // 2
                self.state = (current[:count], current[count:])
            else:
                self.state = (current, current)

    class ShortChain:
        def __init__(self, outs, at_once):
            self.state = tuple(outs)
            self.stages = ["head"] if at_once else ["core", "side"]
            self.stages += ["half", "both"]
            self.stages += [f"s{bit}" for bit in range(3, peer_bits)] + ["back"]
            self.done = 0

        @property
        def open(self):
            return self.done < len(self.stages)

        def start(self):
            stage = self.stages[self.done]
            state = self.state
            if stage == "head":
                self.got = tuple(swap(state[k], k) for k in (2, 3, 1))
                self.kept = state[0]
            elif stage == "core":
                self.got = tuple(swap(state[k], 1) for k in (1, 3))
            elif stage == "side":
                self.got = (swap(state[1], 2),)
                self.kept = state[0]
            elif stage == "half":
                self.got = (move(state[1], "s0"),)
                self.kept = state[0]
            elif stage == "both":
                self.got = tuple(swap(state[0], k, "seq") for k in (4, 6, 2))
                self.kept = state[0]
            else:
                self.got = (move(state[0], "s0" if stage == "back" else stage),)
                self.kept = state[0]

        def absorb(self):
            stage = self.stages[self.done]
            self.done += 1
            if stage == "back":
                self.ends = [self.kept, self.got[0]]
                return
            if stage == "core":
                self.state = (add(self.state[0], self.got[0]), add(self.state[2], self.got[1]))
                return
            got = [array.astype(F32) for array in self.got]
            current = self.kept.astype(F32) + got[-1]
            if len(got) == 3:
                current = current + (got[0] + got[1])
            current = current.astype(BF16)
            if self.stages[self.done] == "half":
                self.state = (current[:1], current[1:])
            else:
                self.state = (current,)

    def mark(meta, chains, new=(), extras=()):
        meta, gots, extras = tie(meta, [chain.got for chain in chains], list(extras))
        for chain, got in zip(chains, gots):
            chain.got = got
            chain.absorb()
        active = [chain for chain in chains if chain.open] + list(new)
        meta, states = tie(meta, [chain.state for chain in [*chains, *new]])
        for chain, state in zip([*chains, *new], states):
            chain.state = state
        for chain in active:
            chain.start()
        return meta, active, extras

    up = Chain(up_stay, up_leave, SIDE_ORDER, ("s1", "s0"))
    down = Chain(down_stay, down_leave, SEQ_ORDER, ("s0", "s1"))
    wide_table = whole((rows, PAIR))
    grads = []

    def attend_back(meta, number):
        first, count = CALLS[number]
        shifted = pl.BlockSpec((1, rows, PAIR), lambda n, p, *_: (n, 0, p + first))
        own = pl.BlockSpec((1, rows, PAIR), lambda n, p, *_: (n, 0, p))
        short = jax.ShapeDtypeStruct((slots, rows, count * PAIR), BF16)
        grads.append(
            call(
                attend_back_kernel,
                "attend_back",
                meta,
                [q, k, v, context_grad, context, context_rest, stats, cos, sin],
                (slots, count),
                [shifted] * 7 + [wide_table] * 2,
                [own] * 3 + [pl.BlockSpec((1, 8, PAIR), lambda n, p, *_: (n, 0, p))],
                [short] * 3 + [jax.ShapeDtypeStruct((slots, 8, count * PAIR), F32)],
                [pltpu.VMEM((PAIR, rows), F32)],
                cost=(40 * work * rows * count // pairs, 18 * work * count // pairs),
            )
        )

    def column_spec(array):
        return pl.BlockSpec((slots, portion, array.shape[-1]), lambda k, m: (0, k ^ m[0], 0))

    def weight_chain(meta, parts, head_count, at_once):
        arrays = [array for part in parts for array in part[:3]]
        shape = (2, 3 * head_count * HD // 2, width)
        outs = call(
            functools.partial(weight_kernel, len(parts), head_count),
            "weight_back",
            meta,
            [*arrays, normed],
            (heads,),
            [column_spec(array) for array in arrays] + [flat],
            [pl.BlockSpec(shape, lambda *_: (0, 0, 0))] * heads,
            [jax.ShapeDtypeStruct(shape, BF16)] * heads,
            [pltpu.VMEM((3 * head_count * heads * HD, width), F32)],
            cost=(2 * work * head_count * heads * HD * 3, 8 * work),
        )
        return ShortChain(outs, at_once)

    def placed(meta, moved, name):
        shape = (slots, heads, portion, width)
        return call(
            functools.partial(place_kernel, heads),
            name,
            meta,
            moved,
            (1,),
            [whole((slots, portion, width))] * heads,
            whole(shape),
            jax.ShapeDtypeStruct(shape, BF16),
            cost=(0, 4 * work),
        ).reshape(total_slots, portion, width)

    now, active, _ = mark(meta, [], [up, down])
    attend_back(now, 0)
    now, active, _ = mark(tie(meta, grads[0])[0], active)
    attend_back(now, 1)
    now, active, _ = mark(tie(meta, grads[1])[0], active)
    now, mixed_two, mixed_three = tie(now, mixed[2], mixed[3])
    mixed_two, mixed_three = swap(mixed_two, 2), swap(mixed_three, 3)
    attend_back(now, 2)
    early = weight_chain(now, grads[:3], 2, False)
    now, active, _ = mark(tie(meta, grads[2], early.state)[0], active, [early])
    attend_back(now, 3)
    now, active, _ = mark(tie(meta, grads[3])[0], active)
    attend_back(now, 4)
    late = weight_chain(now, grads[3:], 1, True)
    now, active, (mixed_two, mixed_three) = mark(
        tie(meta, late.state)[0], active, [late], [mixed_two, mixed_three]
    )
    mixed_moved = [mixed[0], swap(mixed[1], 1), mixed_two, mixed_three]

    own_codons = lax.dynamic_index_in_dim(
        codons.reshape(slots, heads, rows), here, 1, keepdims=False
    )
    own_owners = lax.dynamic_index_in_dim(
        owners.reshape(slots, heads), here, 1, keepdims=False
    )
    live = jnp.arange(rows)[None, :] < own_lengths[:, None]
    matches = (own_codons[:, :, None] == jnp.arange(CODONS)[None, None, :]) & live[:, :, None]
    counts = jnp.sum(matches.astype(F32), axis=1)
    owned = (own_owners[None, :] == jnp.arange(peers)[:, None]).astype(F32)
    counts = jnp.sum(owned[:, :, None] * counts[None, :, :], axis=1).reshape(-1)
    free = (VECTOR_ROWS - named - heads) * width
    counts = jnp.pad(counts, (0, free - counts.shape[0])).reshape(-1, width)
    vec_in = jnp.concatenate([feed_vec[: named + heads], counts], axis=0)

    columns = len(CALLS)

    def input_back(meta, first, number, vec_in):
        chosen = pl.BlockSpec((slots, portion, width), lambda k, m: (0, (k + first) ^ m[0], 0))
        specs = []
        for part in grads:
            specs += [
                pl.BlockSpec(
                    (slots, portion, array.shape[-1]), lambda k, m: (0, (k + first) ^ m[0], 0)
                )
                for array in part[:3]
            ]
            specs += [whole(part[3].shape)]
        out = call(
            functools.partial(input_kernel, number, columns, first == 3),
            "input_back",
            meta,
            [
                *toks[first : first + number],
                *squares,
                *[array for part in grads for array in part],
                vec,
                vec_in,
                middle_grad,
            ],
            (number,),
            [ANYWHERE] * (number + PIECES) + specs + [vec_spec, vec_spec, chosen],
            [ANYWHERE] * number + [vec_out],
            [piece] * number + [vector],
            [
                pair_buffer,
                pair_buffer,
                square_buffer,
                square_buffer,
                square_buffer,
                row_sems,
                two,
                three_heads,
            ],
            cost=(6 * work * width * number // heads, 16 * work * number // heads),
        )
        return out[:number], out[number]

    (piece_three,), all_vec = input_back(now, 3, 1, vec_in)
    now, piece_three = tie(tie(meta, all_vec)[0], piece_three)
    piece_three = swap(piece_three, 3)
    now, active, _ = mark(now, active)
    (piece_two,), all_vec = input_back(now, 2, 1, all_vec)
    now, piece_two = tie(tie(meta, all_vec)[0], piece_two)
    piece_two = swap(piece_two, 2)
    now, active, (piece_three,) = mark(now, active, extras=[piece_three])
    (piece_own, piece_core), all_vec = input_back(now, 0, 2, all_vec)
    now, all_vec, piece_core = tie(now, all_vec, piece_core)
    piece_core = swap(piece_core, 1)
    now, active, (piece_two,) = mark(now, active, extras=[piece_two])
    while up.open or down.open:
        now, active, _ = mark(now, active)
    now, all_vec = tie(now, all_vec)
    one_vec = swap(all_vec, 1, "seq")
    mixed_out = placed(now, mixed_moved, "place_mixed")
    now, active, (one_vec, mixed_out) = mark(now, active, extras=[one_vec, mixed_out])
    all_vec = all_vec + one_vec
    seq_vec = [swap(all_vec, k, "seq") for k in (4, 6, 2)]
    input_out = placed(now, [piece_own, piece_core, piece_two, piece_three], "place_input")
    grad_up = call(
        functools.partial(unpack_up_kernel, up.first_bits),
        "unpack_up",
        now,
        up.ends,
        (1,),
        [whole(array.shape) for array in up.ends],
        whole((width, width)),
        jax.ShapeDtypeStruct((width, width), F32),
        cost=(0, 6 * width * width),
    )
    now, active, (*seq_vec, input_out, grad_up) = mark(
        now, active, extras=[*seq_vec, input_out, grad_up]
    )
    all_vec = (all_vec + seq_vec[2]) + (seq_vec[0] + seq_vec[1])
    for bit in range(3, peer_bits):
        all_vec = all_vec + swap(all_vec, 1 << bit, "seq")
    own_vec = [swap(all_vec, k) for k in (2, 3, 1)]
    grad_down, grad_out = call(
        functools.partial(unpack_down_kernel, down.first_bits),
        "unpack_down",
        now,
        down.ends,
        (1,),
        [whole(array.shape) for array in down.ends],
        [whole((width, width)), whole((part_width, width))],
        [
            jax.ShapeDtypeStruct((width, width), F32),
            jax.ShapeDtypeStruct((part_width, width), F32),
        ],
        [pltpu.VMEM((width, width), F32)],
        cost=(0, 8 * width * width),
    )
    while active:
        now, active, _ = mark(now, active)
    own_vec, grad_down = tie(own_vec, grad_down)
    all_vec = (all_vec + own_vec[2]) + (own_vec[0] + own_vec[1])

    def half_spec(array):
        return whole(array.shape)

    head_shape = jax.ShapeDtypeStruct((part_width, width), F32)
    sources = [*early.ends, *late.ends]
    grad_q, grad_k, grad_v = call(
        functools.partial(unpack_heads_kernel, 2),
        "unpack_heads",
        meta,
        sources,
        (1,),
        [half_spec(array) for array in sources],
        [whole((part_width, width))] * 3,
        [head_shape] * 3,
        cost=(0, 6 * width * width),
    )

    by_head = lax.dynamic_index_in_dim(
        all_vec[:3].reshape(3, HEADS_EACH, heads, HD), here, 2, keepdims=False
    ).reshape(3, part_width)
    sums = lax.dynamic_slice_in_dim(all_vec[3:named], here * part_width, part_width, 1)
    dbq, dbk, dbv = [by_head[i] for i in range(3)]
    dbo, dbd, dg1, db1, dg2, db2 = [sums[i] for i in range(named - 3)]
    grad_b_up = lax.dynamic_index_in_dim(all_vec[named:], here, 0, keepdims=False)
    histogram = lax.dynamic_slice_in_dim(
        all_vec[named + heads :].reshape(1, -1), position * CODONS, CODONS, 1
    ).astype(jnp.int32)
    return (
        mixed_out,
        input_out,
        dg1,
        db1,
        grad_q,
        dbq,
        grad_k,
        dbk,
        grad_v,
        dbv,
        grad_out,
        dbo,
        dg2,
        db2,
        grad_up,
        grad_b_up,
        grad_down,
        dbd,
        histogram,
    )


def solution(mesh):
    return jax.shard_map(
        local,
        mesh=mesh,
        in_specs=(
            P("seq", "head", None),
            P("seq", "head", None),
            P("seq"),
            P("seq"),
            P("seq", None),
            P("head"),
            P("head"),
            P("head", None),
            P("head"),
            P("head", None),
            P("head"),
            P("head", None),
            P("head"),
            P("head", None),
            P("head"),
            P("head"),
            P("head"),
            P(None, "head"),
            P("head"),
            P("head", None),
            P("head"),
        ),
        out_specs=(
            P("seq", "head", None),
            P("seq", "head", None),
            P("head"),
            P("head"),
            P("head", None),
            P("head"),
            P("head", None),
            P("head"),
            P("head", None),
            P("head"),
            P("head", None),
            P("head"),
            P("head"),
            P("head"),
            P(None, "head"),
            P("head"),
            P("head", None),
            P("head"),
            P("seq", None),
        ),
        check_vma=False,
    )
```

time: 2270 us -> 550 us (0.24); the launches traced: 2240 us -> 545 us
  waiting for transfers between devices: 1060 us -> 89.7 us
  local copies, waits for them, and re-layouts: 511 us -> 26.7 us
  Pallas kernels: 0 us -> 348 us
  matrix products: 264 us -> 0 us
  blocking collectives: 178 us -> 0 us
  other arithmetic: 171 us -> 24.4 us
  starting transfers between devices: 31 us -> 54.5 us
    unnamed x9 -> x0, waiting for transfers between devices: 383 us -> none
    pallas_call x0 -> x20, Pallas kernels: none -> 348 us  [call(): pl.pallas_call(kernel, grid_spec=pltpu.PrefetchScalarGridSpec(num_scalar_...]
    ppermute x18 -> x58, waiting for transfers between devices: 358 us -> 89.7 us  [swap(): return lax.ppermute(array, axis, [(i, i ^ bits) for i in range(size)])]
    dot_general x54 -> x0, matrix products: 264 us -> none  [the longest x1 35.5 us: local(): jnp.einsum('rd,fd->rf', out_grad_low, down_weight, preferred_element_type...]
    dynamic_update_slice x20 -> x0, local copies, waits for them, and re-layouts: 204 us -> none  [butterfly(): lax.dynamic_update_index_in_dim(shaped, arriving.reshape(leaving.shape),...]
    psum x2 -> x0, waiting for transfers between devices: 181 us -> none  [the longest x1 181 us: local(): second_norm_gradient = lax.psum(norm_two_part, 'head')]
    all_gather x3 -> x0, waiting for transfers between devices: 140 us -> none  [the longest x1 71.3 us: local(): lax.all_gather(middle_part.reshape(owned_row_count, portion_rows, width),...]
    psum x1 -> x0, blocking collectives: 124 us -> none  [local(): lax.psum((grad_ln1_gain, grad_ln1_bias, grad_w_query, grad_b_query, grad_...]
  transfers between devices with their start and end apart: 25 -> 58, of which waited for: 15 -> 15; matrix products, arithmetic and copies ran while one was open for 18% -> 4% of each run, Pallas kernels for 0% -> 41%
where the time goes in v1:
time: 550 us; the launch traced here: 545 us
  Pallas kernels  348 us (63%)
  waiting for transfers between devices  89.7 us (16%)
  starting transfers between devices  54.5 us (10%)
  local copies, waits for them, and re-layouts  26.7 us (5%)
  other arithmetic  24.4 us (4%)
    pallas_call x20, Pallas kernels, call(): pl.pallas_call(kernel, grid_spec=pltpu.PrefetchScalarGridSpec(num_scalar_...  348 us
    ppermute x58, waiting for transfers between devices, swap(): return lax.ppermute(array, axis, [(i, i ^ bits) for i in range(size)])  89.7 us
    ppermute x58, starting transfers between devices, swap(): return lax.ppermute(array, axis, [(i, i ^ bits) for i in range(size)])  54.5 us
    unnamed x114, local copies, waits for them, and re-layouts  11 us
  transfers between devices with their start and end apart: 58, of which 15 were waited for; matrix products, arithmetic and copies ran while one was open for 4% of the time, Pallas kernels for 41%

profile of v1, /device:TPU:0, one launch (start us, length us, event | category | flops | bytes accessed | tf_op | source)
XLA Modules:
  0.0 545.0 jit_solution(807975505269604657)
XLA Ops:
  17.6 26.0 %collective-permute-done.refs_2_.refs_6_.refs_10_.refs_3_.refs_0_.refs_4_ = bf16[912,768]{1,0:T(8,128)(2,1)S(1)} collective-permute-done((bf16[912,768]{1,0:T(8,128)(2,1)}, bf16[912,768]{1,0:T(8,128)(2,1)S(1)}, u32[]{:S(2)}, u32[]{:S(2)}) %collective-permute-start) | collective-permute-done | bytes 1400864 | tf_op jit(solution)/shard_map/ppermute | solution.py:877
  50.6 8.3 %collective-permute-done.4.refs_3_.refs_0_ = bf16[512,768]{1,0:T(8,128)(2,1)} collective-permute-done((bf16[512,768]{1,0:T(8,128)(2,1)}, bf16[512,768]{1,0:T(8,128)(2,1)}, u32[]{:S(2)}, u32[]{:S(2)}) %collective-permute-start.4) | collective-permute-done | bytes 786464 | tf_op jit(solution)/shard_map/ppermute | solution.py:877
  69.0 18.3 %project.1 = (bf16[2,1024,768]{2,1,0:T(8,128)(2,1)}, bf16[2,1024,768]{2,1,0:T(8,128)(2,1)}, bf16[2,1024,768]{2,1,0:T(8,128)(2,1)}, bf16[2,1024,768]{2,1,0:T(8,128)(2,1)}) custom-call(s32[4]{0:T(128)} %pad_add_fusion.meta, bf16[512,768]{1,0:T(8,128)(2,1)} %bitcast.46, bf16[512,768]{1,0:T(8,128)(2,1)} %copy-done.6, bf16[912,768]{1,0:T(8,128)(2,1)} %copy-done, ...), custom_call_target="tpu_custom_call" | custom-call | flops 1 | bytes 1 | tf_op jit(solution)/shard_map/project/pallas_call | solution.py:820
  94.8 20.5 %attend.2 = (bf16[2,1024,768]{2,1,0:T(8,128)(2,1)}, bf16[2,1024,768]{2,1,0:T(8,128)(2,1)}, bf16[2,1024,768]{2,1,0:T(8,128)(2,1)}) custom-call(s32[4]{0:T(128)} %pad_add_fusion.meta, bf16[2,1024,768]{2,1,0:T(8,128)(2,1)} %get-tuple-element.252.q_ref, bf16[2,1024,768]{2,1,0:T(8,128)(2,1)} %get-tuple-element.253.k_ref, ...), custom_call_target="tpu_custom_call" | custom-call | flops 1 | bytes 1 | tf_op jit(solution)/shard_map/attend/pallas_call | solution.py:820
  117.8 20.4 %attend.3 = (bf16[2,1024,768]{2,1,0:T(8,128)(2,1)}, bf16[2,1024,768]{2,1,0:T(8,128)(2,1)}, bf16[2,1024,768]{2,1,0:T(8,128)(2,1)}) custom-call(s32[4]{0:T(128)} %pad_add_fusion.meta, bf16[2,1024,768]{2,1,0:T(8,128)(2,1)} %get-tuple-element.252.q_ref, ...), custom_call_target="tpu_custom_call", output_to_operand_aliasing={{0}: (4, {}), {1}: (5, {}), {2}: (6, {})} | custom-call | flops 1 | bytes 1 | tf_op jit(solution)/shard_map/attend/pallas_call | solution.py:820
  138.3 124.9 %feed.1 = (bf16[2,256,768]{2,1,0:T(8,128)(2,1)}, bf16[2,256,768]{2,1,0:T(8,128)(2,1)}, bf16[2,256,768]{2,1,0:T(8,128)(2,1)}, bf16[2,256,768]{2,1,0:T(8,128)(2,1)...) custom-call(s32[4]{0:T(128)} %pad_add_fusion.meta, ...), custom_call_target="tpu_custom_call" | custom-call | flops 1 | bytes 1 | tf_op jit(solution)/shard_map/feed/pallas_call | solution.py:820
  263.8 15.7 %attend_back.5 = (bf16[2,1024,128]{2,1,0:T(8,128)(2,1)}, bf16[2,1024,128]{2,1,0:T(8,128)(2,1)}, bf16[2,1024,128]{2,1,0:T(8,128)(2,1)}, f32[2,8,128]{2,1,0:T(8,128)}) custom-call(s32[4]{0:T(128)} %pad_add_fusion.meta, bf16[2,1024,768]{2,1,0:T(8,128)(2,1)} %get-tuple-element.252.q_ref, bf16[2,1024,768]{2,1,0:T(8,128)(2,1)} %get-tuple-element.253.k_ref, ...), custom_call_target="tpu_custom_call" | custom-call | flops 1 | bytes 1 | tf_op jit(solution)/shard_map/attend_back/pallas_call | solution.py:820
  289.0 27.8 %attend_back.6 = (bf16[2,1024,256]{2,1,0:T(8,128)(2,1)}, bf16[2,1024,256]{2,1,0:T(8,128)(2,1)}, bf16[2,1024,256]{2,1,0:T(8,128)(2,1)}, f32[2,8,256]{2,1,0:T(8,128)}) custom-call(s32[4]{0:T(128)} %pad_add_fusion.meta, bf16[2,1024,768]{2,1,0:T(8,128)(2,1)} %get-tuple-element.252.q_ref, bf16[2,1024,768]{2,1,0:T(8,128)(2,1)} %get-tuple-element.253.k_ref, ...), custom_call_target="tpu_custom_call" | custom-call | flops 1 | bytes 1 | tf_op jit(solution)/shard_map/attend_back/pallas_call | solution.py:820
  317.0 4.9 collective-permute-done.18
  328.5 15.5 %attend_back.7 = (bf16[2,1024,128]{2,1,0:T(8,128)(2,1)}, bf16[2,1024,128]{2,1,0:T(8,128)(2,1)}, bf16[2,1024,128]{2,1,0:T(8,128)(2,1)}, f32[2,8,128]{2,1,0:T(8,128)}) custom-call(s32[4]{0:T(128)} %pad_add_fusion.meta, bf16[2,1024,768]{2,1,0:T(8,128)(2,1)} %get-tuple-element.252.q_ref, bf16[2,1024,768]{2,1,0:T(8,128)(2,1)} %get-tuple-element.253.k_ref, ...), custom_call_target="tpu_custom_call" | custom-call | flops 1 | bytes 1 | tf_op jit(solution)/shard_map/attend_back/pallas_call | solution.py:820
  344.0 11.1 %weight_back.2 = (bf16[2,192,768]{2,1,0:T(8,128)(2,1)}, bf16[2,192,768]{2,1,0:T(8,128)(2,1)}, bf16[2,192,768]{2,1,0:T(8,128)(2,1)}, bf16[2,192,768]{2,1,0:T(8,128)(2,1)}) custom-call(s32[4]{0:T(128)} %pad_add_fusion.meta, bf16[2,1024,128]{2,1,0:T(8,128)(2,1)} %get-tuple-element.275.refs_0_.refs_7_.refs_8_, ...), custom_call_target="tpu_custom_call" | custom-call | flops 1 | bytes 1 | tf_op jit(solution)/shard_map/weight_back/pallas_call | solution.py:820
  359.2 15.5 %attend_back.8 = (bf16[2,1024,128]{2,1,0:T(8,128)(2,1)}, bf16[2,1024,128]{2,1,0:T(8,128)(2,1)}, bf16[2,1024,128]{2,1,0:T(8,128)(2,1)}, f32[2,8,128]{2,1,0:T(8,128)}) custom-call(s32[4]{0:T(128)} %pad_add_fusion.meta, bf16[2,1024,768]{2,1,0:T(8,128)(2,1)} %get-tuple-element.252.q_ref, bf16[2,1024,768]{2,1,0:T(8,128)(2,1)} %get-tuple-element.253.k_ref, ...), custom_call_target="tpu_custom_call" | custom-call | flops 1 | bytes 1 | tf_op jit(solution)/shard_map/attend_back/pallas_call | solution.py:820
  381.4 15.5 %attend_back.9 = (bf16[2,1024,128]{2,1,0:T(8,128)(2,1)}, bf16[2,1024,128]{2,1,0:T(8,128)(2,1)}, bf16[2,1024,128]{2,1,0:T(8,128)(2,1)}, f32[2,8,128]{2,1,0:T(8,128)}) custom-call(s32[4]{0:T(128)} %pad_add_fusion.meta, bf16[2,1024,768]{2,1,0:T(8,128)(2,1)} %get-tuple-element.252.q_ref, bf16[2,1024,768]{2,1,0:T(8,128)(2,1)} %get-tuple-element.253.k_ref, ...), custom_call_target="tpu_custom_call" | custom-call | flops 1 | bytes 1 | tf_op jit(solution)/shard_map/attend_back/pallas_call | solution.py:820
  396.9 7.8 %weight_back.3 = (bf16[2,96,768]{2,1,0:T(8,128)(2,1)}, bf16[2,96,768]{2,1,0:T(8,128)(2,1)}, bf16[2,96,768]{2,1,0:T(8,128)(2,1)}, bf16[2,96,768]{2,1,0:T(8,128)(2,1)}) custom-call(s32[4]{0:T(128)} %pad_add_fusion.meta, bf16[2,1024,128]{2,1,0:T(8,128)(2,1)} %get-tuple-element.322.refs_0_.refs_19_.refs_20_, ...), custom_call_target="tpu_custom_call" | custom-call | flops 1 | bytes 1 | tf_op jit(solution)/shard_map/weight_back/pallas_call | solution.py:820
  404.7 6.2 %collective-permute-done.25 = bf16[1,192,768]{2,1,0:T(8,128)(2,1)S(1)} collective-permute-done((bf16[1,192,768]{2,1,0:T(8,128)(2,1)S(1)}, bf16[1,192,768]{2,1,0:T(8,128)(2,1)S(1)}, u32[]{:S(2)}, u32[]{:S(2)}) %collective-permute-start.25) | collective-permute-done | bytes 294944 | tf_op jit(solution)/shard_map/ppermute | solution.py:877
  419.0 5.0 collective-permute-done.30
  425.1 9.9 %input_back.3 = (bf16[2,256,768]{2,1,0:T(8,128)(2,1)}, f32[16,768]{1,0:T(8,128)}) custom-call(s32[4]{0:T(128)} %pad_add_fusion.meta, bf16[512,768]{1,0:T(8,128)(2,1)} %collective-permute-done.4.refs_3_.refs_0_, bf16[784,768]{1,0:T(8,128)(2,1)} %copy-done.1, bf16[784,768]{1,0:T(8,128)(2,1)} %copy-done.2, bf16[912,768]{1,0:T(8,128)(2,1)} %copy-done, ...), custom_call_target="tpu_custom_call" | custom-call | flops 1 | bytes 1 | tf_op jit(solution)/shard_map/input_back/pallas_call | solution.py:820
  443.0 15.9 %collective-permute-done.41 = bf16[1,96,768]{2,1,0:T(8,128)(2,1)S(1)} collective-permute-done((bf16[1,96,768]{2,1,0:T(8,128)(2,1)S(1)}, bf16[1,96,768]{2,1,0:T(8,128)(2,1)S(1)}, u32[]{:S(2)}, u32[]{:S(2)}) %collective-permute-start.41) | collective-permute-done | bytes 147488 | tf_op jit(solution)/shard_map/ppermute | solution.py:877
  461.6 4.7 collective-permute-start.40
  466.2 9.7 %input_back.4 = (bf16[2,256,768]{2,1,0:T(8,128)(2,1)}, f32[16,768]{1,0:T(8,128)}) custom-call(s32[4]{0:T(128)} %pad_add_fusion.meta, bf16[912,768]{1,0:T(8,128)(2,1)} %copy-done, bf16[784,768]{1,0:T(8,128)(2,1)} %copy-done.1, bf16[784,768]{1,0:T(8,128)(2,1)} %copy-done.2, bf16[912,768]{1,0:T(8,128)(2,1)} %copy-done, ...), custom_call_target="tpu_custom_call" | custom-call | flops 1 | bytes 1 | tf_op jit(solution)/shard_map/input_back/pallas_call | solution.py:820
  479.2 13.2 %input_back.5 = (bf16[2,256,768]{2,1,0:T(8,128)(2,1)}, bf16[2,256,768]{2,1,0:T(8,128)(2,1)}, f32[16,768]{1,0:T(8,128)}) custom-call(s32[4]{0:T(128)} %pad_add_fusion.meta, bf16[512,768]{1,0:T(8,128)(2,1)} %bitcast.48, bf16[512,768]{1,0:T(8,128)(2,1)} %copy-done.6, bf16[784,768]{1,0:T(8,128)(2,1)} %copy-done.1, bf16[784,768]{1,0:T(8,128)(2,1)} %copy-done.2, ...), custom_call_target="tpu_custom_call" | custom-call | flops 1 | bytes 1 | tf_op jit(solution)/shard_map/input_back/pallas_call | solution.py:820
  497.6 9.3 %collective-permute-done.44 = bf16[1,96,768]{2,1,0:T(8,128)(2,1)S(1)} collective-permute-done((bf16[1,96,768]{2,1,0:T(8,128)(2,1)S(1)}, bf16[1,96,768]{2,1,0:T(8,128)(2,1)S(1)}, u32[]{:S(2)}, u32[]{:S(2)}) %collective-permute-start.44) | collective-permute-done | bytes 147488 | tf_op jit(solution)/shard_map/ppermute | solution.py:877
  506.9 5.1 collective-permute-done.46
  514.2 4.5 place_mixed.1
  (294 shorter events, 127.6 us)
Async XLA Ops:
  8.9 34.7 %collective-permute-start = (bf16[912,768]{1,0:T(8,128)(2,1)}, bf16[912,768]{1,0:T(8,128)(2,1)S(1)}, u32[]{:S(2)}, u32[]{:S(2)}) collective-permute-start(bf16[912,768]{1,0:T(8,128)(2,1)} %get-tuple-element.236), channel_id=1, source_target_pairs={{0,2},{1,3},{2,0},{3,1},{4,6},{5,7},{6,4},{7,5},{8,10},{9,11},{10,... | collective-permute-start | bytes 4202504 | tf_op jit(solution)/shard_map/ppermute | solution.py:877
  12.3 46.6 %collective-permute-start.4 = (bf16[512,768]{1,0:T(8,128)(2,1)}, bf16[512,768]{1,0:T(8,128)(2,1)}, u32[]{:S(2)}, u32[]{:S(2)}) collective-permute-start(bf16[512,768]{1,0:T(8,128)(2,1)} %bitcast.59), channel_id=1, source_target_pairs={{0,3},{1,2},{2,1},{3,0},{4,7},{5,6},{6,5},{7,4},{8,11},{9,10},{10,... | collective-permute-start | bytes 2359304 | tf_op jit(solution)/shard_map/ppermute | solution.py:877
  59.0 28.8 %collective-permute-start.8 = (bf16[2,384,768]{2,1,0:T(8,128)(2,1)}, bf16[2,384,768]{2,1,0:T(8,128)(2,1)}, u32[]{:S(2)}, u32[]{:S(2)}) collective-permute-start(bf16[2,384,768]{2,1,0:T(8,128)(2,1)} %fusion), channel_id=1, source_target_pairs={{0,2},{1,3},{2,0},{3,1},{4,6},{5,7},{6,4},{7,5},{8,10},{9,11},{10,... | collective-permute-start | bytes 3538952 | tf_op jit(solution)/shard_map/ppermute | solution.py:877
  87.8 28.1 %collective-permute-start.9 = (bf16[2,384,768]{2,1,0:T(8,128)(2,1)}, bf16[2,384,768]{2,1,0:T(8,128)(2,1)S(1)}, u32[]{:S(2)}, u32[]{:S(2)}) collective-permute-start(bf16[2,384,768]{2,1,0:T(8,128)(2,1)} %collective-permute-done.8.refs_16_), channel_id=1, source_target_pairs={{0,4},{4,0},{8,12},{12,8},{16,20},{20,16},{24,28},{28,24},{1,5},{5... | collective-permute-start | bytes 3538952 | tf_op jit(solution)/shard_map/ppermute | solution.py:877
  89.5 48.7 %collective-permute-start.12 = (bf16[2,768,768]{2,1,0:T(8,128)(2,1)S(1)}, bf16[2,768,768]{2,1,0:T(8,128)(2,1)}, u32[]{:S(2)}, u32[]{:S(2)}) collective-permute-start(bf16[2,768,768]{2,1,0:T(8,128)(2,1)S(1)} %copy-done.5), channel_id=1, source_target_pairs={{0,1},{1,0},{2,3},{3,2},{4,5},{5,4},{6,7},{7,6},{8,9},{9,8},{10,11... | collective-permute-start | bytes 7077896 | tf_op jit(solution)/shard_map/ppermute | solution.py:877
  93.1 22.2 %collective-permute-start.10 = (bf16[512,768]{1,0:T(8,128)(2,1)}, bf16[512,768]{1,0:T(8,128)(2,1)}, u32[]{:S(2)}, u32[]{:S(2)}) collective-permute-start(bf16[512,768]{1,0:T(8,128)(2,1)} %bitcast.12), channel_id=1, source_target_pairs={{0,2},{1,3},{2,0},{3,1},{4,6},{5,7},{6,4},{7,5},{8,10},{9,11},{10,... | collective-permute-start | bytes 2359304 | tf_op jit(solution)/shard_map/ppermute | solution.py:877
  94.6 43.6 %collective-permute-start.13 = (bf16[2,384,768]{2,1,0:T(8,128)(2,1)}, bf16[2,384,768]{2,1,0:T(8,128)(2,1)}, u32[]{:S(2)}, u32[]{:S(2)}) collective-permute-start(bf16[2,384,768]{2,1,0:T(8,128)(2,1)} %collective-permute-done.8.refs_16_), channel_id=1, source_target_pairs={{0,1},{1,0},{2,3},{3,2},{4,5},{5,4},{6,7},{7,6},{8,9},{9,8},{10,11... | collective-permute-start | bytes 3538952 | tf_op jit(solution)/shard_map/ppermute | solution.py:877
  115.9 22.4 %collective-permute-start.14 = (bf16[2,384,768]{2,1,0:T(8,128)(2,1)S(1)}, bf16[2,384,768]{2,1,0:T(8,128)(2,1)}, u32[]{:S(2)}, u32[]{:S(2)}) collective-permute-start(bf16[2,384,768]{2,1,0:T(8,128)(2,1)S(1)} %collective-permute-done.9.refs_17_), channel_id=1, source_target_pairs={{0,1},{1,0},{2,3},{3,2},{4,5},{5,4},{6,7},{7,6},{8,9},{9,8},{10,11... | collective-permute-start | bytes 3538952 | tf_op jit(solution)/shard_map/ppermute | solution.py:877
  115.9 22.3 %collective-permute-start.11 = (bf16[512,768]{1,0:T(8,128)(2,1)}, bf16[512,768]{1,0:T(8,128)(2,1)}, u32[]{:S(2)}, u32[]{:S(2)}) collective-permute-start(bf16[512,768]{1,0:T(8,128)(2,1)} %bitcast.62), channel_id=1, source_target_pairs={{0,3},{1,2},{2,1},{3,0},{4,7},{5,6},{6,5},{7,4},{8,11},{9,10},{10,... | collective-permute-start | bytes 2359304 | tf_op jit(solution)/shard_map/ppermute | solution.py:877
  287.1 34.7 %collective-permute-start.18 = (bf16[4,240,768]{2,1,0:T(8,128)(2,1)S(1)}, bf16[4,240,768]{2,1,0:T(8,128)(2,1)}, u32[]{:S(2)}, u32[]{:S(2)}) collective-permute-start(bf16[4,240,768]{2,1,0:T(8,128)(2,1)S(1)} %get-tuple-element.294), channel_id=1, source_target_pairs={{0,4},{4,0},{8,12},{12,8},{16,20},{20,16},{24,28},{28,24},{1,5},{5... | collective-permute-start | bytes 4423688 | tf_op jit(solution)/shard_map/ppermute | solution.py:877
  288.6 28.4 %collective-permute-start.17 = (bf16[4,192,768]{2,1,0:T(8,128)(2,1)}, bf16[4,192,768]{2,1,0:T(8,128)(2,1)}, u32[]{:S(2)}, u32[]{:S(2)}) collective-permute-start(bf16[4,192,768]{2,1,0:T(8,128)(2,1)} %get-tuple-element.293), channel_id=1, source_target_pairs={{0,2},{1,3},{2,0},{3,1},{4,6},{5,7},{6,4},{7,5},{8,10},{9,11},{10,... | collective-permute-start | bytes 3538952 | tf_op jit(solution)/shard_map/ppermute | solution.py:877
  325.3 29.7 %collective-permute-start.20 = (bf16[2,240,768]{2,1,0:T(8,128)(2,1)S(1)}, bf16[2,240,768]{2,1,0:T(8,128)(2,1)S(1)}, u32[]{:S(2)}, u32[]{:S(2)}) collective-permute-start(bf16[2,240,768]{2,1,0:T(8,128)(2,1)S(1)} %get-tuple-element.315), channel_id=1, source_target_pairs={{0,8},{4,12},{8,0},{12,4},{16,24},{20,28},{24,16},{28,20},{1,9},{5... | collective-permute-start | bytes 2211848 | tf_op jit(solution)/shard_map/ppermute | solution.py:877
  327.0 28.1 %collective-permute-start.19 = (bf16[2,192,768]{2,1,0:T(8,128)(2,1)S(1)}, bf16[2,192,768]{2,1,0:T(8,128)(2,1)S(1)}, u32[]{:S(2)}, u32[]{:S(2)}) collective-permute-start(bf16[2,192,768]{2,1,0:T(8,128)(2,1)S(1)} %get-tuple-element.314), channel_id=1, source_target_pairs={{0,4},{4,0},{8,12},{12,8},{16,20},{20,16},{24,28},{28,24},{1,5},{5... | collective-permute-start | bytes 1769480 | tf_op jit(solution)/shard_map/ppermute | solution.py:877
  357.6 47.1 %collective-permute-start.28 = (bf16[2,256,768]{2,1,0:T(8,128)(2,1)}, bf16[2,256,768]{2,1,0:T(8,128)(2,1)S(1)}, u32[]{:S(2)}, u32[]{:S(2)}) collective-permute-start(bf16[2,256,768]{2,1,0:T(8,128)(2,1)} %get-tuple-element.352), channel_id=1, source_target_pairs={{0,2},{1,3},{2,0},{3,1},{4,6},{5,7},{6,4},{7,5},{8,10},{9,11},{10,... | collective-permute-start | bytes 2359304 | tf_op jit(solution)/shard_map/ppermute | solution.py:877
  374.7 30.0 %collective-permute-start.29 = (bf16[2,256,768]{2,1,0:T(8,128)(2,1)}, bf16[2,256,768]{2,1,0:T(8,128)(2,1)}, u32[]{:S(2)}, u32[]{:S(2)}) collective-permute-start(bf16[2,256,768]{2,1,0:T(8,128)(2,1)} %get-tuple-element.353), channel_id=1, source_target_pairs={{0,3},{1,2},{2,1},{3,0},{4,7},{5,6},{6,5},{7,4},{8,11},{9,10},{10,... | collective-permute-start | bytes 2359304 | tf_op jit(solution)/shard_map/ppermute | solution.py:877
  377.7 36.0 %collective-permute-start.27 = (bf16[2,192,768]{2,1,0:T(8,128)(2,1)S(1)}, bf16[2,192,768]{2,1,0:T(8,128)(2,1)}, u32[]{:S(2)}, u32[]{:S(2)}) collective-permute-start(bf16[2,192,768]{2,1,0:T(8,128)(2,1)S(1)} %add_convert_fusion.6), channel_id=1, source_target_pairs={{0,2},{1,3},{2,0},{3,1},{4,6},{5,7},{6,4},{7,5},{8,10},{9,11},{10,... | collective-permute-start | bytes 1769480 | tf_op jit(solution)/shard_map/ppermute | solution.py:877
  378.1 32.8 %collective-permute-start.26 = (bf16[1,240,768]{2,1,0:T(8,128)(2,1)S(1)}, bf16[1,240,768]{2,1,0:T(8,128)(2,1)S(1)}, u32[]{:S(2)}, u32[]{:S(2)}) collective-permute-start(bf16[1,240,768]{2,1,0:T(8,128)(2,1)S(1)} %add_convert_fusion.10), channel_id=1, source_target_pairs={{0,16},{4,20},{8,24},{12,28},{16,0},{20,4},{24,8},{28,12},{1,17},{... | collective-permute-start | bytes 1105928 | tf_op jit(solution)/shard_map/ppermute | solution.py:877
  380.7 30.2 %collective-permute-start.25 = (bf16[1,192,768]{2,1,0:T(8,128)(2,1)S(1)}, bf16[1,192,768]{2,1,0:T(8,128)(2,1)S(1)}, u32[]{:S(2)}, u32[]{:S(2)}) collective-permute-start(bf16[1,192,768]{2,1,0:T(8,128)(2,1)S(1)} %add_convert_fusion.15), channel_id=1, source_target_pairs={{0,16},{4,20},{8,24},{12,28},{16,0},{20,4},{24,8},{28,12},{1,17},{... | collective-permute-start | bytes 884744 | tf_op jit(solution)/shard_map/ppermute | solution.py:877
  435.0 42.8 %collective-permute-start.42 = (bf16[2,256,768]{2,1,0:T(8,128)(2,1)}, bf16[2,256,768]{2,1,0:T(8,128)(2,1)S(1)}, u32[]{:S(2)}, u32[]{:S(2)}) collective-permute-start(bf16[2,256,768]{2,1,0:T(8,128)(2,1)} %get-tuple-element.395), channel_id=1, source_target_pairs={{0,3},{1,2},{2,1},{3,0},{4,7},{5,6},{6,5},{7,4},{8,11},{9,10},{10,... | collective-permute-start | bytes 2359304 | tf_op jit(solution)/shard_map/ppermute | solution.py:877
  437.8 39.9 %collective-permute-start.37 = (bf16[2,240,768]{2,1,0:T(8,128)(2,1)S(1)}, bf16[2,240,768]{2,1,0:T(8,128)(2,1)S(1)}, u32[]{:S(2)}, u32[]{:S(2)}) collective-permute-start(bf16[2,240,768]{2,1,0:T(8,128)(2,1)S(1)} %pad_maximum_fusion.1.near), channel_id=1, source_target_pairs={{0,8},{4,12},{8,0},{12,4},{16,24},{20,28},{24,16},{28,20},{1,9},{5... | collective-permute-start | bytes 2211848 | tf_op jit(solution)/shard_map/ppermute | solution.py:877
  438.3 23.2 %collective-permute-start.38 = (bf16[1,192,768]{2,1,0:T(8,128)(2,1)S(1)}, bf16[1,192,768]{2,1,0:T(8,128)(2,1)S(1)}, u32[]{:S(2)}, u32[]{:S(2)}) collective-permute-start(bf16[1,192,768]{2,1,0:T(8,128)(2,1)S(1)} %add_convert_fusion.13), channel_id=1, source_target_pairs={{0,16},{4,20},{8,24},{12,28},{16,0},{20,4},{24,8},{28,12},{1,17},{... | collective-permute-start | bytes 884744 | tf_op jit(solution)/shard_map/ppermute | solution.py:877
  440.9 36.8 %collective-permute-start.36 = (bf16[2,192,768]{2,1,0:T(8,128)(2,1)S(1)}, bf16[2,192,768]{2,1,0:T(8,128)(2,1)}, u32[]{:S(2)}, u32[]{:S(2)}) collective-permute-start(bf16[2,192,768]{2,1,0:T(8,128)(2,1)S(1)} %pad_maximum_fusion.2.near), channel_id=1, source_target_pairs={{0,4},{4,0},{8,12},{12,8},{16,20},{20,16},{24,28},{28,24},{1,5},{5... | collective-permute-start | bytes 1769480 | tf_op jit(solution)/shard_map/ppermute | solution.py:877
  477.7 36.5 %collective-permute-start.50 = (bf16[2,256,768]{2,1,0:T(8,128)(2,1)}, bf16[2,256,768]{2,1,0:T(8,128)(2,1)}, u32[]{:S(2)}, u32[]{:S(2)}) collective-permute-start(bf16[2,256,768]{2,1,0:T(8,128)(2,1)} %get-tuple-element.421), channel_id=1, source_target_pairs={{0,1},{1,0},{2,3},{3,2},{4,5},{5,4},{6,7},{7,6},{8,9},{9,8},{10,11... | collective-permute-start | bytes 2359304 | tf_op jit(solution)/shard_map/ppermute | solution.py:877
  492.4 33.4 %collective-permute-start.54 = (bf16[2,256,768]{2,1,0:T(8,128)(2,1)}, bf16[2,256,768]{2,1,0:T(8,128)(2,1)S(1)}, u32[]{:S(2)}, u32[]{:S(2)}) collective-permute-start(bf16[2,256,768]{2,1,0:T(8,128)(2,1)} %get-tuple-element.429), channel_id=1, source_target_pairs={{0,1},{1,0},{2,3},{3,2},{4,5},{5,4},{6,7},{7,6},{8,9},{9,8},{10,11... | collective-permute-start | bytes 2359304 | tf_op jit(solution)/shard_map/ppermute | solution.py:877
  (85 other events, 839.9 us)

commit v2 on v1

--- a/solution.py
+++ b/solution.py
@@ -1293,7 +1293,7 @@
             ]
             specs += [whole(part[3].shape)]
         out = call(
-            functools.partial(input_kernel, number, columns, first == 3),
+            functools.partial(input_kernel, number, columns, True),
             "input_back",
             meta,
             [
@@ -1322,24 +1322,18 @@
         )
         return out[:number], out[number]
 
-    (piece_three,), all_vec = input_back(now, 3, 1, vec_in)
-    now, piece_three = tie(tie(meta, all_vec)[0], piece_three)
-    piece_three = swap(piece_three, 3)
-    now, active, _ = mark(now, active)
-    (piece_two,), all_vec = input_back(now, 2, 1, all_vec)
-    now, piece_two = tie(tie(meta, all_vec)[0], piece_two)
-    piece_two = swap(piece_two, 2)
-    now, active, (piece_three,) = mark(now, active, extras=[piece_three])
-    (piece_own, piece_core), all_vec = input_back(now, 0, 2, all_vec)
-    now, all_vec, piece_core = tie(now, all_vec, piece_core)
-    piece_core = swap(piece_core, 1)
-    now, active, (piece_two,) = mark(now, active, extras=[piece_two])
+    pieces, all_vec = input_back(now, 0, heads, vec_in)
+    now, active, _ = mark(tie(meta, all_vec)[0], active)
+    now, all_vec, pieces = tie(now, all_vec, pieces)
+    piece_three, piece_two = swap(pieces[3], 3), swap(pieces[2], 2)
+    piece_own, piece_core = pieces[0], swap(pieces[1], 1)
+    one_vec = swap(all_vec, 1, "seq")
+    mixed_out = placed(now, mixed_moved, "place_mixed")
+    now, active, (piece_three, piece_two, one_vec, mixed_out) = mark(
+        now, active, extras=[piece_three, piece_two, one_vec, mixed_out]
+    )
     while up.open or down.open:
         now, active, _ = mark(now, active)
-    now, all_vec = tie(now, all_vec)
-    one_vec = swap(all_vec, 1, "seq")
-    mixed_out = placed(now, mixed_moved, "place_mixed")
-    now, active, (one_vec, mixed_out) = mark(now, active, extras=[one_vec, mixed_out])
     all_vec = all_vec + one_vec
     seq_vec = [swap(all_vec, k, "seq") for k in (4, 6, 2)]
     input_out = placed(now, [piece_own, piece_core, piece_two, piece_three], "place_input")

time: 550 us -> 550 us (level)
  Pallas kernels: 348 us -> 334 us
  waiting for transfers between devices: 89.7 us -> 101 us
    pallas_call x20 -> x18, Pallas kernels: 348 us -> 334 us  [call(): pl.pallas_call(kernel, grid_spec=pltpu.PrefetchScalarGridSpec(num_scalar_...]
    ppermute x58, waiting for transfers between devices: 89.7 us -> 101 us  [swap(): return lax.ppermute(array, axis, [(i, i ^ bits) for i in range(size)])]
    unnamed x114 -> x122, local copies, waits for them, and re-layouts: 11 us -> 12.8 us
  transfers between devices with their start and end apart: 58 -> 58, of which waited for: 15 -> 17; matrix products, arithmetic and copies ran while one was open for 4% -> 5% of each run, Pallas kernels for 41% -> 38%
where the time goes in v2:
time: 550 us; the launch traced here: 545 us
  Pallas kernels  334 us (61%)
  waiting for transfers between devices  101 us (18%)
  starting transfers between devices  53.4 us (10%)
  local copies, waits for them, and re-layouts  27.8 us (5%)
  other arithmetic  26.8 us (5%)
    pallas_call x18, Pallas kernels, call(): pl.pallas_call(kernel, grid_spec=pltpu.PrefetchScalarGridSpec(num_scalar_...  334 us
    ppermute x58, waiting for transfers between devices, swap(): return lax.ppermute(array, axis, [(i, i ^ bits) for i in range(size)])  101 us
    ppermute x58, starting transfers between devices, swap(): return lax.ppermute(array, axis, [(i, i ^ bits) for i in range(size)])  53.4 us
    unnamed x122, local copies, waits for them, and re-layouts  12.8 us
    convert_element_type x12, other arithmetic, add(): return (one.astype(F32) + other.astype(F32)).astype(BF16)  12.1 us
  transfers between devices with their start and end apart: 58, of which 17 were waited for; matrix products, arithmetic and copies ran while one was open for 5% of the time, Pallas kernels for 38%

profile of v2, /device:TPU:0, one launch (start us, length us, event | category | flops | bytes accessed | tf_op | source)
XLA Modules:
  0.0 544.7 jit_solution(15881989318850134718)
XLA Ops:
  17.7 25.9 %collective-permute-done.refs_2_.refs_6_.refs_10_ = bf16[912,768]{1,0:T(8,128)(2,1)S(1)} collective-permute-done((bf16[912,768]{1,0:T(8,128)(2,1)}, bf16[912,768]{1,0:T(8,128)(2,1)S(1)}, u32[]{:S(2)}, u32[]{:S(2)}) %collective-permute-start) | collective-permute-done | bytes 1400864 | tf_op jit(solution)/shard_map/ppermute | solution.py:877
  50.6 8.3 %collective-permute-done.4.refs_3_ = bf16[512,768]{1,0:T(8,128)(2,1)} collective-permute-done((bf16[512,768]{1,0:T(8,128)(2,1)}, bf16[512,768]{1,0:T(8,128)(2,1)}, u32[]{:S(2)}, u32[]{:S(2)}) %collective-permute-start.4) | collective-permute-done | bytes 786464 | tf_op jit(solution)/shard_map/ppermute | solution.py:877
  69.0 18.2 %project.1 = (bf16[2,1024,768]{2,1,0:T(8,128)(2,1)}, bf16[2,1024,768]{2,1,0:T(8,128)(2,1)}, bf16[2,1024,768]{2,1,0:T(8,128)(2,1)}, bf16[2,1024,768]{2,1,0:T(8,128)(2,1)}) custom-call(s32[4]{0:T(128)} %pad_add_fusion.meta, bf16[512,768]{1,0:T(8,128)(2,1)} %bitcast.46, bf16[512,768]{1,0:T(8,128)(2,1)} %copy-done.5, bf16[912,768]{1,0:T(8,128)(2,1)} %copy-done, ...), custom_call_target="tpu_custom_call" | custom-call | flops 1 | bytes 1 | tf_op jit(solution)/shard_map/project/pallas_call | solution.py:820
  94.8 20.4 %attend.2 = (bf16[2,1024,768]{2,1,0:T(8,128)(2,1)}, bf16[2,1024,768]{2,1,0:T(8,128)(2,1)}, bf16[2,1024,768]{2,1,0:T(8,128)(2,1)}) custom-call(s32[4]{0:T(128)} %pad_add_fusion.meta, bf16[2,1024,768]{2,1,0:T(8,128)(2,1)} %get-tuple-element.243.q_ref, bf16[2,1024,768]{2,1,0:T(8,128)(2,1)} %get-tuple-element.244.k_ref, ...), custom_call_target="tpu_custom_call" | custom-call | flops 1 | bytes 1 | tf_op jit(solution)/shard_map/attend/pallas_call | solution.py:820
  117.8 20.4 %attend.3 = (bf16[2,1024,768]{2,1,0:T(8,128)(2,1)}, bf16[2,1024,768]{2,1,0:T(8,128)(2,1)}, bf16[2,1024,768]{2,1,0:T(8,128)(2,1)}) custom-call(s32[4]{0:T(128)} %pad_add_fusion.meta, bf16[2,1024,768]{2,1,0:T(8,128)(2,1)} %get-tuple-element.243.q_ref, ...), custom_call_target="tpu_custom_call", output_to_operand_aliasing={{0}: (4, {}), {1}: (5, {}), {2}: (6, {})} | custom-call | flops 1 | bytes 1 | tf_op jit(solution)/shard_map/attend/pallas_call | solution.py:820
  138.3 124.8 %feed.1 = (bf16[2,256,768]{2,1,0:T(8,128)(2,1)}, bf16[2,256,768]{2,1,0:T(8,128)(2,1)}, bf16[2,256,768]{2,1,0:T(8,128)(2,1)}, bf16[2,256,768]{2,1,0:T(8,128)(2,1)...) custom-call(s32[4]{0:T(128)} %pad_add_fusion.meta, ...), custom_call_target="tpu_custom_call" | custom-call | flops 1 | bytes 1 | tf_op jit(solution)/shard_map/feed/pallas_call | solution.py:820
  263.7 15.7 %attend_back.5 = (bf16[2,1024,128]{2,1,0:T(8,128)(2,1)}, bf16[2,1024,128]{2,1,0:T(8,128)(2,1)}, bf16[2,1024,128]{2,1,0:T(8,128)(2,1)}, f32[2,8,128]{2,1,0:T(8,128)}) custom-call(s32[4]{0:T(128)} %pad_add_fusion.meta, bf16[2,1024,768]{2,1,0:T(8,128)(2,1)} %get-tuple-element.243.q_ref, bf16[2,1024,768]{2,1,0:T(8,128)(2,1)} %get-tuple-element.244.k_ref, ...), custom_call_target="tpu_custom_call" | custom-call | flops 1 | bytes 1 | tf_op jit(solution)/shard_map/attend_back/pallas_call | solution.py:820
  288.9 27.8 %attend_back.6 = (bf16[2,1024,256]{2,1,0:T(8,128)(2,1)}, bf16[2,1024,256]{2,1,0:T(8,128)(2,1)}, bf16[2,1024,256]{2,1,0:T(8,128)(2,1)}, f32[2,8,256]{2,1,0:T(8,128)}) custom-call(s32[4]{0:T(128)} %pad_add_fusion.meta, bf16[2,1024,768]{2,1,0:T(8,128)(2,1)} %get-tuple-element.243.q_ref, bf16[2,1024,768]{2,1,0:T(8,128)(2,1)} %get-tuple-element.244.k_ref, ...), custom_call_target="tpu_custom_call" | custom-call | flops 1 | bytes 1 | tf_op jit(solution)/shard_map/attend_back/pallas_call | solution.py:820
  316.9 4.9 collective-permute-done.18
  328.4 15.5 %attend_back.7 = (bf16[2,1024,128]{2,1,0:T(8,128)(2,1)}, bf16[2,1024,128]{2,1,0:T(8,128)(2,1)}, bf16[2,1024,128]{2,1,0:T(8,128)(2,1)}, f32[2,8,128]{2,1,0:T(8,128)}) custom-call(s32[4]{0:T(128)} %pad_add_fusion.meta, bf16[2,1024,768]{2,1,0:T(8,128)(2,1)} %get-tuple-element.243.q_ref, bf16[2,1024,768]{2,1,0:T(8,128)(2,1)} %get-tuple-element.244.k_ref, ...), custom_call_target="tpu_custom_call" | custom-call | flops 1 | bytes 1 | tf_op jit(solution)/shard_map/attend_back/pallas_call | solution.py:820
  343.8 10.9 %weight_back.2 = (bf16[2,192,768]{2,1,0:T(8,128)(2,1)}, bf16[2,192,768]{2,1,0:T(8,128)(2,1)}, bf16[2,192,768]{2,1,0:T(8,128)(2,1)}, bf16[2,192,768]{2,1,0:T(8,128)(2,1)}) custom-call(s32[4]{0:T(128)} %pad_add_fusion.meta, bf16[2,1024,128]{2,1,0:T(8,128)(2,1)} %get-tuple-element.266.refs_0_.refs_10_, ...), custom_call_target="tpu_custom_call" | custom-call | flops 1 | bytes 1 | tf_op jit(solution)/shard_map/weight_back/pallas_call | solution.py:820
  358.9 15.5 %attend_back.8 = (bf16[2,1024,128]{2,1,0:T(8,128)(2,1)}, bf16[2,1024,128]{2,1,0:T(8,128)(2,1)}, bf16[2,1024,128]{2,1,0:T(8,128)(2,1)}, f32[2,8,128]{2,1,0:T(8,128)}) custom-call(s32[4]{0:T(128)} %pad_add_fusion.meta, bf16[2,1024,768]{2,1,0:T(8,128)(2,1)} %get-tuple-element.243.q_ref, bf16[2,1024,768]{2,1,0:T(8,128)(2,1)} %get-tuple-element.244.k_ref, ...), custom_call_target="tpu_custom_call" | custom-call | flops 1 | bytes 1 | tf_op jit(solution)/shard_map/attend_back/pallas_call | solution.py:820
  383.0 15.9 %attend_back.9 = (bf16[2,1024,128]{2,1,0:T(8,128)(2,1)}, bf16[2,1024,128]{2,1,0:T(8,128)(2,1)}, bf16[2,1024,128]{2,1,0:T(8,128)(2,1)}, f32[2,8,128]{2,1,0:T(8,128)}) custom-call(s32[4]{0:T(128)} %pad_add_fusion.meta, bf16[2,1024,768]{2,1,0:T(8,128)(2,1)} %get-tuple-element.243.q_ref, bf16[2,1024,768]{2,1,0:T(8,128)(2,1)} %get-tuple-element.244.k_ref, ...), custom_call_target="tpu_custom_call" | custom-call | flops 1 | bytes 1 | tf_op jit(solution)/shard_map/attend_back/pallas_call | solution.py:820
  398.9 7.6 %weight_back.3 = (bf16[2,96,768]{2,1,0:T(8,128)(2,1)}, bf16[2,96,768]{2,1,0:T(8,128)(2,1)}, bf16[2,96,768]{2,1,0:T(8,128)(2,1)}, bf16[2,96,768]{2,1,0:T(8,128)(2,1)}) custom-call(s32[4]{0:T(128)} %pad_add_fusion.meta, bf16[2,1024,128]{2,1,0:T(8,128)(2,1)} %get-tuple-element.313.refs_0_.refs_22_, bf16[2,1024,128]{2,1,0:T(8,128)(2,1)} %get-tuple-element.314.refs_1_.refs_23_, ...), custom_call_target="tpu_custom_call" | custom-call | flops 1 | bytes 1 | tf_op jit(solution)/shard_map/weight_back/pallas_call | solution.py:820
  406.6 6.0 %collective-permute-done.25 = bf16[1,192,768]{2,1,0:T(8,128)(2,1)S(1)} collective-permute-done((bf16[1,192,768]{2,1,0:T(8,128)(2,1)S(1)}, bf16[1,192,768]{2,1,0:T(8,128)(2,1)S(1)}, u32[]{:S(2)}, u32[]{:S(2)}) %collective-permute-start.25) | collective-permute-done | bytes 294944 | tf_op jit(solution)/shard_map/ppermute | solution.py:877
  417.9 5.2 collective-permute-done.30
  424.1 19.6 %input_back.1 = (bf16[2,256,768]{2,1,0:T(8,128)(2,1)}, bf16[2,256,768]{2,1,0:T(8,128)(2,1)}, bf16[2,256,768]{2,1,0:T(8,128)(2,1)}, bf16[2,256,768]{2,1,0:T(8,128)(2,1)}, f32[16,768]{1,0:T(8,128)}) custom-call(s32[4]{0:T(128)} %pad_add_fusion.meta, bf16[512,768]{1,0:T(8,128)(2,1)} %bitcast.48, bf16[512,768]{1,0:T(8,128)(2,1)} %copy-done.5, ...), custom_call_target="tpu_custom_call" | custom-call | flops 1 | bytes 1 | tf_op jit(solution)/shard_map/input_back/pallas_call | solution.py:820
  459.5 6.2 %collective-permute-done.38 = bf16[1,192,768]{2,1,0:T(8,128)(2,1)S(1)} collective-permute-done((bf16[1,192,768]{2,1,0:T(8,128)(2,1)S(1)}, bf16[1,192,768]{2,1,0:T(8,128)(2,1)S(1)}, u32[]{:S(2)}, u32[]{:S(2)}) %collective-permute-start.38) | collective-permute-done | bytes 294944 | tf_op jit(solution)/shard_map/ppermute | solution.py:877
  466.2 15.4 %collective-permute-done.39 = bf16[1,192,768]{2,1,0:T(8,128)(2,1)S(1)} collective-permute-done((bf16[1,192,768]{2,1,0:T(8,128)(2,1)S(1)}, bf16[1,192,768]{2,1,0:T(8,128)(2,1)S(1)}, u32[]{:S(2)}, u32[]{:S(2)}) %collective-permute-start.39) | collective-permute-done | bytes 294944 | tf_op jit(solution)/shard_map/ppermute | solution.py:877
  481.5 11.1 %collective-permute-done.40 = bf16[1,192,768]{2,1,0:T(8,128)(2,1)S(1)} collective-permute-done((bf16[1,192,768]{2,1,0:T(8,128)(2,1)S(1)}, bf16[1,192,768]{2,1,0:T(8,128)(2,1)S(1)}, u32[]{:S(2)}, u32[]{:S(2)}) %collective-permute-start.40) | collective-permute-done | bytes 294944 | tf_op jit(solution)/shard_map/ppermute | solution.py:877
  493.4 4.4 place_mixed.1
  505.8 5.5 %collective-permute-done.50 = f32[16,768]{1,0:T(8,128)S(1)} collective-permute-done((f32[16,768]{1,0:T(8,128)S(1)}, f32[16,768]{1,0:T(8,128)S(1)}, u32[]{:S(2)}, u32[]{:S(2)}) %collective-permute-start.50) | collective-permute-done | bytes 49184 | tf_op jit(solution)/shard_map/ppermute | solution.py:877
  524.0 4.4 place_input.1
  532.3 4.4 unpack_down.1
  (300 shorter events, 129.1 us)
Async XLA Ops:
  8.9 34.7 %collective-permute-start = (bf16[912,768]{1,0:T(8,128)(2,1)}, bf16[912,768]{1,0:T(8,128)(2,1)S(1)}, u32[]{:S(2)}, u32[]{:S(2)}) collective-permute-start(bf16[912,768]{1,0:T(8,128)(2,1)} %get-tuple-element.227), channel_id=1, source_target_pairs={{0,2},{1,3},{2,0},{3,1},{4,6},{5,7},{6,4},{7,5},{8,10},{9,11},{10,... | collective-permute-start | bytes 4202504 | tf_op jit(solution)/shard_map/ppermute | solution.py:877
  12.3 46.6 %collective-permute-start.4 = (bf16[512,768]{1,0:T(8,128)(2,1)}, bf16[512,768]{1,0:T(8,128)(2,1)}, u32[]{:S(2)}, u32[]{:S(2)}) collective-permute-start(bf16[512,768]{1,0:T(8,128)(2,1)} %bitcast.59), channel_id=1, source_target_pairs={{0,3},{1,2},{2,1},{3,0},{4,7},{5,6},{6,5},{7,4},{8,11},{9,10},{10,... | collective-permute-start | bytes 2359304 | tf_op jit(solution)/shard_map/ppermute | solution.py:877
  59.0 28.8 %collective-permute-start.8 = (bf16[2,384,768]{2,1,0:T(8,128)(2,1)}, bf16[2,384,768]{2,1,0:T(8,128)(2,1)}, u32[]{:S(2)}, u32[]{:S(2)}) collective-permute-start(bf16[2,384,768]{2,1,0:T(8,128)(2,1)} %fusion), channel_id=1, source_target_pairs={{0,2},{1,3},{2,0},{3,1},{4,6},{5,7},{6,4},{7,5},{8,10},{9,11},{10,... | collective-permute-start | bytes 3538952 | tf_op jit(solution)/shard_map/ppermute | solution.py:877
  87.8 28.0 %collective-permute-start.9 = (bf16[2,384,768]{2,1,0:T(8,128)(2,1)}, bf16[2,384,768]{2,1,0:T(8,128)(2,1)S(1)}, u32[]{:S(2)}, u32[]{:S(2)}) collective-permute-start(bf16[2,384,768]{2,1,0:T(8,128)(2,1)} %collective-permute-done.8.refs_16_), channel_id=1, source_target_pairs={{0,4},{4,0},{8,12},{12,8},{16,20},{20,16},{24,28},{28,24},{1,5},{5... | collective-permute-start | bytes 3538952 | tf_op jit(solution)/shard_map/ppermute | solution.py:877
  89.5 48.7 %collective-permute-start.12 = (bf16[2,768,768]{2,1,0:T(8,128)(2,1)S(1)}, bf16[2,768,768]{2,1,0:T(8,128)(2,1)}, u32[]{:S(2)}, u32[]{:S(2)}) collective-permute-start(bf16[2,768,768]{2,1,0:T(8,128)(2,1)S(1)} %copy-done.4), channel_id=1, source_target_pairs={{0,1},{1,0},{2,3},{3,2},{4,5},{5,4},{6,7},{7,6},{8,9},{9,8},{10,11... | collective-permute-start | bytes 7077896 | tf_op jit(solution)/shard_map/ppermute | solution.py:877
  94.6 43.7 %collective-permute-start.13 = (bf16[2,384,768]{2,1,0:T(8,128)(2,1)}, bf16[2,384,768]{2,1,0:T(8,128)(2,1)}, u32[]{:S(2)}, u32[]{:S(2)}) collective-permute-start(bf16[2,384,768]{2,1,0:T(8,128)(2,1)} %collective-permute-done.8.refs_16_), channel_id=1, source_target_pairs={{0,1},{1,0},{2,3},{3,2},{4,5},{5,4},{6,7},{7,6},{8,9},{9,8},{10,11... | collective-permute-start | bytes 3538952 | tf_op jit(solution)/shard_map/ppermute | solution.py:877
  287.0 34.7 %collective-permute-start.18 = (bf16[4,240,768]{2,1,0:T(8,128)(2,1)S(1)}, bf16[4,240,768]{2,1,0:T(8,128)(2,1)}, u32[]{:S(2)}, u32[]{:S(2)}) collective-permute-start(bf16[4,240,768]{2,1,0:T(8,128)(2,1)S(1)} %get-tuple-element.285), channel_id=1, source_target_pairs={{0,4},{4,0},{8,12},{12,8},{16,20},{20,16},{24,28},{28,24},{1,5},{5... | collective-permute-start | bytes 4423688 | tf_op jit(solution)/shard_map/ppermute | solution.py:877
  288.5 28.4 %collective-permute-start.17 = (bf16[4,192,768]{2,1,0:T(8,128)(2,1)}, bf16[4,192,768]{2,1,0:T(8,128)(2,1)}, u32[]{:S(2)}, u32[]{:S(2)}) collective-permute-start(bf16[4,192,768]{2,1,0:T(8,128)(2,1)} %get-tuple-element.284), channel_id=1, source_target_pairs={{0,2},{1,3},{2,0},{3,1},{4,6},{5,7},{6,4},{7,5},{8,10},{9,11},{10,... | collective-permute-start | bytes 3538952 | tf_op jit(solution)/shard_map/ppermute | solution.py:877
  325.2 29.5 %collective-permute-start.20 = (bf16[2,240,768]{2,1,0:T(8,128)(2,1)S(1)}, bf16[2,240,768]{2,1,0:T(8,128)(2,1)S(1)}, u32[]{:S(2)}, u32[]{:S(2)}) collective-permute-start(bf16[2,240,768]{2,1,0:T(8,128)(2,1)S(1)} %get-tuple-element.306), channel_id=1, source_target_pairs={{0,8},{4,12},{8,0},{12,4},{16,24},{20,28},{24,16},{28,20},{1,9},{5... | collective-permute-start | bytes 2211848 | tf_op jit(solution)/shard_map/ppermute | solution.py:877
  326.9 27.9 %collective-permute-start.19 = (bf16[2,192,768]{2,1,0:T(8,128)(2,1)S(1)}, bf16[2,192,768]{2,1,0:T(8,128)(2,1)S(1)}, u32[]{:S(2)}, u32[]{:S(2)}) collective-permute-start(bf16[2,192,768]{2,1,0:T(8,128)(2,1)S(1)} %get-tuple-element.305), channel_id=1, source_target_pairs={{0,4},{4,0},{8,12},{12,8},{16,20},{20,16},{24,28},{28,24},{1,5},{5... | collective-permute-start | bytes 1769480 | tf_op jit(solution)/shard_map/ppermute | solution.py:877
  357.3 49.3 %collective-permute-start.28 = (bf16[2,256,768]{2,1,0:T(8,128)(2,1)}, bf16[2,256,768]{2,1,0:T(8,128)(2,1)S(1)}, u32[]{:S(2)}, u32[]{:S(2)}) collective-permute-start(bf16[2,256,768]{2,1,0:T(8,128)(2,1)} %get-tuple-element.343), channel_id=1, source_target_pairs={{0,2},{1,3},{2,0},{3,1},{4,6},{5,7},{6,4},{7,5},{8,10},{9,11},{10,... | collective-permute-start | bytes 2359304 | tf_op jit(solution)/shard_map/ppermute | solution.py:877
  374.4 32.2 %collective-permute-start.29 = (bf16[2,256,768]{2,1,0:T(8,128)(2,1)}, bf16[2,256,768]{2,1,0:T(8,128)(2,1)}, u32[]{:S(2)}, u32[]{:S(2)}) collective-permute-start(bf16[2,256,768]{2,1,0:T(8,128)(2,1)} %get-tuple-element.344), channel_id=1, source_target_pairs={{0,3},{1,2},{2,1},{3,0},{4,7},{5,6},{6,5},{7,4},{8,11},{9,10},{10,... | collective-permute-start | bytes 2359304 | tf_op jit(solution)/shard_map/ppermute | solution.py:877
  378.9 34.5 %collective-permute-start.27 = (bf16[2,192,768]{2,1,0:T(8,128)(2,1)S(1)}, bf16[2,192,768]{2,1,0:T(8,128)(2,1)}, u32[]{:S(2)}, u32[]{:S(2)}) collective-permute-start(bf16[2,192,768]{2,1,0:T(8,128)(2,1)S(1)} %add_convert_fusion.6), channel_id=1, source_target_pairs={{0,2},{1,3},{2,0},{3,1},{4,6},{5,7},{6,4},{7,5},{8,10},{9,11},{10,... | collective-permute-start | bytes 1769480 | tf_op jit(solution)/shard_map/ppermute | solution.py:877
  379.7 32.8 %collective-permute-start.26 = (bf16[1,240,768]{2,1,0:T(8,128)(2,1)S(1)}, bf16[1,240,768]{2,1,0:T(8,128)(2,1)S(1)}, u32[]{:S(2)}, u32[]{:S(2)}) collective-permute-start(bf16[1,240,768]{2,1,0:T(8,128)(2,1)S(1)} %add_convert_fusion.10), channel_id=1, source_target_pairs={{0,16},{4,20},{8,24},{12,28},{16,0},{20,4},{24,8},{28,12},{1,17},{... | collective-permute-start | bytes 1105928 | tf_op jit(solution)/shard_map/ppermute | solution.py:877
  382.3 30.2 %collective-permute-start.25 = (bf16[1,192,768]{2,1,0:T(8,128)(2,1)S(1)}, bf16[1,192,768]{2,1,0:T(8,128)(2,1)S(1)}, u32[]{:S(2)}, u32[]{:S(2)}) collective-permute-start(bf16[1,192,768]{2,1,0:T(8,128)(2,1)S(1)} %add_convert_fusion.15), channel_id=1, source_target_pairs={{0,16},{4,20},{8,24},{12,28},{16,0},{20,4},{24,8},{28,12},{1,17},{... | collective-permute-start | bytes 884744 | tf_op jit(solution)/shard_map/ppermute | solution.py:877
  415.4 30.4 %collective-permute-start.31 = (bf16[1,240,768]{2,1,0:T(8,128)(2,1)S(1)}, bf16[1,240,768]{2,1,0:T(8,128)(2,1)S(1)}, u32[]{:S(2)}, u32[]{:S(2)}) collective-permute-start(bf16[1,240,768]{2,1,0:T(8,128)(2,1)S(1)} %add_convert_fusion.9), channel_id=1, source_target_pairs={{0,4},{4,0},{8,12},{12,8},{16,20},{20,16},{24,28},{28,24},{1,5},{5... | collective-permute-start | bytes 1105928 | tf_op jit(solution)/shard_map/ppermute | solution.py:877
  416.0 27.7 %collective-permute-start.32 = (bf16[1,192,768]{2,1,0:T(8,128)(2,1)S(1)}, bf16[1,192,768]{2,1,0:T(8,128)(2,1)S(1)}, u32[]{:S(2)}, u32[]{:S(2)}) collective-permute-start(bf16[1,192,768]{2,1,0:T(8,128)(2,1)S(1)} %get-tuple-element.360), channel_id=1, source_target_pairs={{0,4},{4,0},{8,12},{12,8},{16,20},{20,16},{24,28},{28,24},{1,5},{5... | collective-permute-start | bytes 884744 | tf_op jit(solution)/shard_map/ppermute | solution.py:877
  417.5 26.8 %collective-permute-start.33 = (bf16[2,96,768]{2,1,0:T(8,128)(2,1)}, bf16[2,96,768]{2,1,0:T(8,128)(2,1)S(1)}, u32[]{:S(2)}, u32[]{:S(2)}) collective-permute-start(bf16[2,96,768]{2,1,0:T(8,128)(2,1)} %get-tuple-element.361), channel_id=1, source_target_pairs={{0,2},{1,3},{2,0},{3,1},{4,6},{5,7},{6,4},{7,5},{8,10},{9,11},{10,... | collective-permute-start | bytes 884744 | tf_op jit(solution)/shard_map/ppermute | solution.py:877
  453.0 44.8 %collective-permute-start.42 = (bf16[2,256,768]{2,1,0:T(8,128)(2,1)}, bf16[2,256,768]{2,1,0:T(8,128)(2,1)S(1)}, u32[]{:S(2)}, u32[]{:S(2)}) collective-permute-start(bf16[2,256,768]{2,1,0:T(8,128)(2,1)} %get-tuple-element.385), channel_id=1, source_target_pairs={{0,3},{1,2},{2,1},{3,0},{4,7},{5,6},{6,5},{7,4},{8,11},{9,10},{10,... | collective-permute-start | bytes 2359304 | tf_op jit(solution)/shard_map/ppermute | solution.py:877
  453.0 44.8 %collective-permute-start.43 = (bf16[2,256,768]{2,1,0:T(8,128)(2,1)}, bf16[2,256,768]{2,1,0:T(8,128)(2,1)S(1)}, u32[]{:S(2)}, u32[]{:S(2)}) collective-permute-start(bf16[2,256,768]{2,1,0:T(8,128)(2,1)} %get-tuple-element.386), channel_id=1, source_target_pairs={{0,2},{1,3},{2,0},{3,1},{4,6},{5,7},{6,4},{7,5},{8,10},{9,11},{10,... | collective-permute-start | bytes 2359304 | tf_op jit(solution)/shard_map/ppermute | solution.py:877
  457.5 40.3 %collective-permute-start.37 = (bf16[2,240,768]{2,1,0:T(8,128)(2,1)S(1)}, bf16[2,240,768]{2,1,0:T(8,128)(2,1)}, u32[]{:S(2)}, u32[]{:S(2)}) collective-permute-start(bf16[2,240,768]{2,1,0:T(8,128)(2,1)S(1)} %pad_maximum_fusion.1.near), channel_id=1, source_target_pairs={{0,8},{4,12},{8,0},{12,4},{16,24},{20,28},{24,16},{28,20},{1,9},{5... | collective-permute-start | bytes 2211848 | tf_op jit(solution)/shard_map/ppermute | solution.py:877
  465.6 32.1 %collective-permute-start.36 = (bf16[2,192,768]{2,1,0:T(8,128)(2,1)S(1)}, bf16[2,192,768]{2,1,0:T(8,128)(2,1)}, u32[]{:S(2)}, u32[]{:S(2)}) collective-permute-start(bf16[2,192,768]{2,1,0:T(8,128)(2,1)S(1)} %pad_maximum_fusion.2.near), channel_id=1, source_target_pairs={{0,4},{4,0},{8,12},{12,8},{16,20},{20,16},{24,28},{28,24},{1,5},{5... | collective-permute-start | bytes 1769480 | tf_op jit(solution)/shard_map/ppermute | solution.py:877
  499.5 28.9 %collective-permute-start.46 = (bf16[1,192,768]{2,1,0:T(8,128)(2,1)S(1)}, bf16[1,192,768]{2,1,0:T(8,128)(2,1)S(1)}, u32[]{:S(2)}, u32[]{:S(2)}) collective-permute-start(bf16[1,192,768]{2,1,0:T(8,128)(2,1)S(1)} %add_convert_fusion.11.near), channel_id=1, source_target_pairs={{0,4},{4,0},{8,12},{12,8},{16,20},{20,16},{24,28},{28,24},{1,5},{5... | collective-permute-start | bytes 884744 | tf_op jit(solution)/shard_map/ppermute | solution.py:877
  500.9 27.5 %collective-permute-start.47 = (bf16[1,96,768]{2,1,0:T(8,128)(2,1)S(1)}, bf16[1,96,768]{2,1,0:T(8,128)(2,1)S(1)}, u32[]{:S(2)}, u32[]{:S(2)}) collective-permute-start(bf16[1,96,768]{2,1,0:T(8,128)(2,1)S(1)} %add_convert_fusion.17), channel_id=1, source_target_pairs={{0,16},{4,20},{8,24},{12,28},{16,0},{20,4},{24,8},{28,12},{1,17},{... | collective-permute-start | bytes 442376 | tf_op jit(solution)/shard_map/ppermute | solution.py:877
  (89 other events, 910.8 us)
